TPU v7x, 768 devices: a whole 4x8x12 slice. The times are simulated.
768 devices in a mesh: row: 24 (over x, z_lo), col: 32 (over z_hi, y, core).
Axes of the slice: x: 4, y: 8, z: 12 (z_hi: 2, z_lo: 6; z = z_hi * 6 + z_lo), core: 2. Of those that a mesh axis runs over, the one named last changes fastest.
Arguments:
- left_factor: bfloat16 [32768, 12288], P('col', 'row'), may hold values from -6 to 6
- left_mask: int32 [256, 96], P('col', 'row'), may hold values from 0 to 1, as said below
- right_factor: bfloat16 [16384, 24576], P('col', 'row'), may hold values from -0.5 to 0.5
- right_mask: int32 [128, 192], P('col', 'row'), may hold values from 0 to 1, as said below
Outputs:
- window_product: bfloat16 [32768, 24576], P('col', 'row')
Inputs may be any that keep to these rules, and one draw needn't show every extreme that they name: `left_mask`: 1 marks an occupied tile; one device's piece of 8 x 4 tiles holds at most 12 ones, and some piece holds exactly 12. `right_mask`: 1 marks an occupied tile; one device's piece of 4 x 8 tiles holds at most 12 ones, and some piece holds exactly 12.
All inputs are finite; a program needn't handle non-finite values.
Results may differ from a plain program's by a relative error of at most 0.001.
Values may be sent and summed in bfloat16 or wider, within the bound.
No kernel may reach another device: no remote copies, remote signals or barrier semaphores. Data moves between devices by JAX's collectives and lax.ppermute only.
A program may use at most 64 MiB of HBM per device.

v0:
```python
import jax
import jax.numpy as jnp
from jax import lax
from jax.sharding import PartitionSpec as P

TILE = 128
STEPS = 4


def shifted(block, axis, distance):
    devices = range(lax.axis_size(axis))
    route = [((i - distance) % len(devices), i) for i in devices]
    return lax.ppermute(block, axis, route)


def apply_mask(tile_mask, block_data):
    expanded = jnp.repeat(jnp.repeat(tile_mask, TILE, axis=0), TILE, axis=1)
    return block_data * expanded.astype(block_data.dtype)


def local(left_factor, left_mask, right_factor, right_mask):
    left_first = apply_mask(left_mask, left_factor)
    right_first = apply_mask(right_mask, right_factor)
    left_now, right_now = (left_first, right_first)
    total = jnp.dot(left_now, right_now, preferred_element_type=jnp.float32)
    for step in range(1, STEPS):
        left_source = left_now
        right_source = right_now
        hops = -1
        left_now = shifted(left_source, "row", hops)
        right_now = shifted(right_source, "col", hops)
        total = total + jnp.dot(left_now, right_now, preferred_element_type=jnp.float32)
    return total.astype(jnp.bfloat16)


def solution(mesh):
    placed = (P("col", "row"), P("col", "row"), P("col", "row"), P("col", "row"))
    return jax.shard_map(
        local, mesh=mesh, in_specs=placed, out_specs=P("col", "row"), check_vma=False
    )
```

profile of v0, /device:TPU:315, one launch (start us, length us, event | category | flops | bytes accessed | tf_op | source)
XLA Modules:
  0.0 196.6 jit_solution(7036950701723340604)
XLA Ops:
  0.0 0.0 copy-start.1
  0.0 0.0 copy-start
  0.0 0.8 convert_element_type.28
  0.8 0.6 broadcast_in_dim.15
  1.4 1.4 bitcast_multiply_fusion
  2.8 2.6 %collective-permute-start.1 = (bf16[512,1024]{1,0:T(8,128)(2,1)S(1)}, bf16[512,1024]{1,0:T(8,128)(2,1)S(1)}, u32[]{:S(2)}, u32[]{:S(2)}) collective-permute-start(bf16[512,1024]{1,0:T(8,128)(2,1)S(1)} %bitcast_multiply_fusion), channel_id=1, source_target_pairs={{1,0},{2,1},{3,2},{4,3},{5,4},{6,5},{7,6},{8,7},{9,8},{10,9},{11,1... | collective-permute-start | bytes 3145736 | tf_op jit(solution)/shard_map/ppermute | solution.py:13
  5.4 0.0 copy-done.1
  5.4 0.1 copy.5
  5.5 2.9 %broadcast_in_dim.13 = bf16[1024,4,128]{2,1,0:T(4,128)(2,1)S(1)} broadcast(bf16[1024,4]{1,0:T(8,128)(2,1)S(1)} %bitcast.18), dimensions={0,1} | broadcast | bytes 1056768 | tf_op jit(solution)/shard_map/broadcast_in_dim | solution.py:17
  8.5 0.0 copy-done
  8.5 0.2 bitcast_multiply_fusion.1
  8.7 1.9 collective-permute-start
  10.6 74.2 %collective-permute-done.1 = bf16[512,1024]{1,0:T(8,128)(2,1)S(1)} collective-permute-done((bf16[512,1024]{1,0:T(8,128)(2,1)S(1)}, bf16[512,1024]{1,0:T(8,128)(2,1)S(1)}, u32[]{:S(2)}, u32[]{:S(2)}) %collective-permute-start.1) | collective-permute-done | bytes 1048608 | tf_op jit(solution)/shard_map/ppermute | solution.py:13
  84.8 1.9 collective-permute-start.3
  86.7 0.0 collective-permute-done
  86.7 1.9 collective-permute-start.2
  88.7 54.8 %collective-permute-done.3 = bf16[512,1024]{1,0:T(8,128)(2,1)S(1)} collective-permute-done((bf16[512,1024]{1,0:T(8,128)(2,1)S(1)}, bf16[512,1024]{1,0:T(8,128)(2,1)S(1)}, u32[]{:S(2)}, u32[]{:S(2)}) %collective-permute-start.3) | collective-permute-done | bytes 1048608 | tf_op jit(solution)/shard_map/ppermute | solution.py:13
  143.5 1.9 collective-permute-start.5
  145.4 0.0 collective-permute-done.2
  145.4 1.9 collective-permute-start.4
  147.3 1.3 fusion
  148.6 1.3 fusion.1
  149.9 1.3 fusion.2
  151.1 42.8 %collective-permute-done.5 = bf16[512,1024]{1,0:T(8,128)(2,1)S(1)} collective-permute-done((bf16[512,1024]{1,0:T(8,128)(2,1)S(1)}, bf16[512,1024]{1,0:T(8,128)(2,1)S(1)}, u32[]{:S(2)}, u32[]{:S(2)}) %collective-permute-start.5) | collective-permute-done | bytes 1048608 | tf_op jit(solution)/shard_map/ppermute | solution.py:13
  193.9 0.0 collective-permute-done.4
  193.9 2.6 %add_convert_fusion = bf16[1024,1024]{1,0:T(8,128)(2,1)} fusion(f32[1024,1024]{1,0:T(8,128)S(1)} %fusion.2, f32[1024,1024]{1,0:T(8,128)S(1)} %fusion, f32[1024,1024]{1,0:T(8,128)S(1)} %fusion.1, bf16[1024,512]{1,0:T(8,128)(2,1)S(1)} %collective-permute-done.4, bf16[512,1024]{1,0:T(8,128)(2,1)S(1)} %collective-permute-done.5), kind=kOutput, calls=%fused_computation | convolution fusion | flops 1077936128 | bytes 16777216 | tf_op jit(solution)/shard_map/dot_general | solution.py:32
  (3 shorter events, 0.1 us)
Async XLA Ops:
  0.0 5.4 %copy-start.1 = (s32[8,4]{0,1:T(4,128)S(1)}, s32[8,4]{0,1:T(4,128)}, u32[]{:S(2)}) copy-start(s32[8,4]{0,1:T(4,128)} %param.5) | copy-start | bytes 388
  0.0 8.5 %copy-start = (bf16[1024,512]{1,0:T(8,128)(2,1)S(1)}, bf16[1024,512]{1,0:T(8,128)(2,1)}, u32[]{:S(2)}) copy-start(bf16[1024,512]{1,0:T(8,128)(2,1)} %param.4) | copy-start | bytes 3145732
  2.8 82.0 %collective-permute-start.1 = (bf16[512,1024]{1,0:T(8,128)(2,1)S(1)}, bf16[512,1024]{1,0:T(8,128)(2,1)S(1)}, u32[]{:S(2)}, u32[]{:S(2)}) collective-permute-start(bf16[512,1024]{1,0:T(8,128)(2,1)S(1)} %bitcast_multiply_fusion), channel_id=1, source_target_pairs={{1,0},{2,1},{3,2},{4,3},{5,4},{6,5},{7,6},{8,7},{9,8},{10,9},{11,1... | collective-permute-start | bytes 3145736 | tf_op jit(solution)/shard_map/ppermute | solution.py:13
  8.7 78.1 %collective-permute-start = (bf16[1024,512]{1,0:T(8,128)(2,1)S(1)}, bf16[1024,512]{1,0:T(8,128)(2,1)S(1)}, u32[]{:S(2)}, u32[]{:S(2)}) collective-permute-start(bf16[1024,512]{1,0:T(8,128)(2,1)S(1)} %bitcast_multiply_fusion.1), channel_id=1, source_target_pairs={{32,0},{64,32},{96,64},{128,96},{160,128},{192,160},{224,192},{256... | collective-permute-start | bytes 3145736 | tf_op jit(solution)/shard_map/ppermute | solution.py:13
  84.8 58.7 %collective-permute-start.3 = (bf16[512,1024]{1,0:T(8,128)(2,1)S(1)}, bf16[512,1024]{1,0:T(8,128)(2,1)S(1)}, u32[]{:S(2)}, u32[]{:S(2)}) collective-permute-start(bf16[512,1024]{1,0:T(8,128)(2,1)S(1)} %collective-permute-done.1), channel_id=1, source_target_pairs={{1,0},{2,1},{3,2},{4,3},{5,4},{6,5},{7,6},{8,7},{9,8},{10,9},{11,1... | collective-permute-start | bytes 3145736 | tf_op jit(solution)/shard_map/ppermute | solution.py:13
  86.7 58.7 %collective-permute-start.2 = (bf16[1024,512]{1,0:T(8,128)(2,1)S(1)}, bf16[1024,512]{1,0:T(8,128)(2,1)S(1)}, u32[]{:S(2)}, u32[]{:S(2)}) collective-permute-start(bf16[1024,512]{1,0:T(8,128)(2,1)S(1)} %collective-permute-done), channel_id=1, source_target_pairs={{32,0},{64,32},{96,64},{128,96},{160,128},{192,160},{224,192},{256... | collective-permute-start | bytes 3145736 | tf_op jit(solution)/shard_map/ppermute | solution.py:13
  143.5 50.5 %collective-permute-start.5 = (bf16[512,1024]{1,0:T(8,128)(2,1)S(1)}, bf16[512,1024]{1,0:T(8,128)(2,1)S(1)}, u32[]{:S(2)}, u32[]{:S(2)}) collective-permute-start(bf16[512,1024]{1,0:T(8,128)(2,1)S(1)} %collective-permute-done.3), channel_id=1, source_target_pairs={{1,0},{2,1},{3,2},{4,3},{5,4},{6,5},{7,6},{8,7},{9,8},{10,9},{11,1... | collective-permute-start | bytes 3145736 | tf_op jit(solution)/shard_map/ppermute | solution.py:13
  145.4 48.5 %collective-permute-start.4 = (bf16[1024,512]{1,0:T(8,128)(2,1)S(1)}, bf16[1024,512]{1,0:T(8,128)(2,1)S(1)}, u32[]{:S(2)}, u32[]{:S(2)}) collective-permute-start(bf16[1024,512]{1,0:T(8,128)(2,1)S(1)} %collective-permute-done.2), channel_id=1, source_target_pairs={{32,0},{64,32},{96,64},{128,96},{160,128},{192,160},{224,192},{256... | collective-permute-start | bytes 3145736 | tf_op jit(solution)/shard_map/ppermute | solution.py:13
where the time goes:
time: 197 us
  waiting for transfers between devices  172 us (87%)
  starting transfers between devices  12.2 us (6%)
  matrix products  6.4 us (3%)
  local copies, waits for them, and re-layouts  3.71 us (2%)
  other arithmetic  2.31 us (1%)
    ppermute x6, waiting for transfers between devices, shifted(): return lax.ppermute(block, axis, route)  172 us
    ppermute x6, starting transfers between devices, shifted(): return lax.ppermute(block, axis, route)  12.2 us
    dot_general x3, matrix products, local(): jnp.dot(left_now, right_now, preferred_element_type=jnp.float32)  5.14 us
  transfers between devices with their start and end apart: 6, of which 3 were waited for; matrix products, arithmetic and copies ran while one was open for 4% of the time, Pallas kernels for 0%

commit v1 on v0

v1 whole, which is shorter than its diff:
```python
import jax
import jax.numpy as jnp
from jax import lax
from jax.experimental import pallas as pl
from jax.experimental.pallas import tpu as pltpu
from jax.sharding import PartitionSpec as P

TILE = 128
TB = 8
KT = 4
OCC = 12
HEAD = 16
PACK = OCC * TILE + HEAD
EMPTY = 64.0
VMEM_LIMIT = 32 * 1024 * 1024


def number_slots(mask_at, tile_rows, tile_cols, slots):
    for j in range(OCC):
        slots[j] = 0
    count = jnp.int32(0)
    for i in range(tile_rows):
        for k in range(tile_cols):
            occupied = mask_at(i, k) != 0

            @pl.when(occupied & (count < OCC))
            def _():
                slots[count] = i * tile_cols + k

            count = count + occupied.astype(jnp.int32)
    return jnp.minimum(count, OCC)


def pack_one(mask_at, source, packed, slots, sem, tile_rows, tile_cols):
    count = number_slots(mask_at, tile_rows, tile_cols, slots)
    copies = []
    for j in range(OCC):
        tile = slots[j]
        i = pl.multiple_of(tile // tile_cols * TILE, TILE)
        k = pl.multiple_of(tile % tile_cols * TILE, TILE)
        copy = pltpu.make_async_copy(
            source.at[pl.ds(i, TILE), pl.ds(k, TILE)],
            packed.at[pl.ds(j * TILE, TILE), :],
            sem.at[j],
        )
        copy.start()
        copies.append(copy)
    lane = lax.broadcasted_iota(jnp.int32, (HEAD, TILE), 1)
    head = jnp.full((HEAD, TILE), EMPTY, jnp.float32)
    for j in range(OCC):
        here = (lane == j) & (j < count)
        head = jnp.where(here, slots[j].astype(jnp.float32), head)
    packed[OCC * TILE : PACK, :] = head.astype(jnp.bfloat16)
    return copies


def pack_kernel(left_mask_across, right_mask, left, right, left_packed, right_packed, slots, sem):
    copies = pack_one(lambda i, k: right_mask[i, k], right, right_packed, slots, sem.at[0], KT, TB)
    copies += pack_one(lambda i, k: left_mask_across[k, i], left, left_packed, slots, sem.at[1], TB, KT)
    for copy in copies:
        copy.wait()


def pack(left_mask, right_mask, left, right):
    smem = pl.BlockSpec(memory_space=pltpu.SMEM)
    hbm = pl.BlockSpec(memory_space=pltpu.HBM)
    vmem = pl.BlockSpec(memory_space=pltpu.VMEM)
    shape = jax.ShapeDtypeStruct((PACK, TILE), jnp.bfloat16)
    return pl.pallas_call(
        pack_kernel,
        out_shape=(shape, shape),
        in_specs=[smem, smem, hbm, hbm],
        out_specs=(vmem, vmem),
        scratch_shapes=[pltpu.SMEM((OCC,), jnp.int32), pltpu.SemaphoreType.DMA((2, OCC))],
        compiler_params=pltpu.CompilerParams(vmem_limit_bytes=VMEM_LIMIT),
        cost_estimate=pl.CostEstimate(flops=0, bytes_accessed=2 * 1024 * 1024, transcendentals=0),
        name="pack",
    )(left_mask.T, right_mask, left, right)


def unpack(packed, dense, tile_cols):
    dense[...] = jnp.zeros_like(dense)
    head = packed[OCC * TILE : PACK, :].astype(jnp.float32).astype(jnp.int32)
    for j in range(OCC):
        tile = head[0, j]

        @pl.when(tile < TB * KT)
        def _():
            i = pl.multiple_of(tile // tile_cols * TILE, TILE)
            k = pl.multiple_of(tile % tile_cols * TILE, TILE)
            dense[pl.ds(i, TILE), pl.ds(k, TILE)] = packed[j * TILE : (j + 1) * TILE, :]


ROWS_AT_ONCE = 256


def step_kernel(*refs, first, last):
    if first:
        left_packed, right_packed, out, left, right = refs
    else:
        total, left_packed, right_packed, out, left, right = refs
    unpack(left_packed, left, KT)
    unpack(right_packed, right, TB)

    @pl.loop(0, TB * TILE // ROWS_AT_ONCE)
    def _(block):
        rows = pl.ds(pl.multiple_of(block * ROWS_AT_ONCE, ROWS_AT_ONCE), ROWS_AT_ONCE)
        part = jnp.dot(left[rows, :], right[...], preferred_element_type=jnp.float32)
        if not first:
            part = total[rows, :] + part
        out[rows, :] = part.astype(out.dtype)


def multiply(total, left_packed, right_packed, last):
    first = total is None
    vmem = pl.BlockSpec(memory_space=pltpu.VMEM)
    args = ([] if first else [total]) + [left_packed, right_packed]
    kind = jnp.bfloat16 if last else jnp.float32
    side = TB * TILE

    def kernel(*refs):
        step_kernel(*refs, first=first, last=last)

    return pl.pallas_call(
        kernel,
        out_shape=jax.ShapeDtypeStruct((side, side), kind),
        in_specs=[vmem] * len(args),
        out_specs=vmem,
        scratch_shapes=[
            pltpu.VMEM((side, KT * TILE), jnp.bfloat16),
            pltpu.VMEM((KT * TILE, side), jnp.bfloat16),
        ],
        compiler_params=pltpu.CompilerParams(vmem_limit_bytes=VMEM_LIMIT),
        cost_estimate=pl.CostEstimate(
            flops=2 * side * side * KT * TILE, bytes_accessed=2 * 1024 * 1024, transcendentals=0
        ),
        name="multiply",
    )(*args)


def shifted(block, axis, distance):
    size = lax.axis_size(axis)
    return lax.ppermute(block, axis, [((i + distance) % size, i) for i in range(size)])


def local(left_factor, left_mask, right_factor, right_mask):
    left, right = pack(left_mask, right_mask, left_factor, right_factor)
    lefts, rights = [left], [right]
    for _ in range(3):
        rights.append(shifted(rights[-1], "col", 1))
        lefts.append(shifted(lefts[-1], "row", 1))
    total = None
    for step in range(4):
        total = multiply(total, lefts[step], rights[step], step == 3)
    return total


def solution(mesh):
    placed = (P("col", "row"), P("col", "row"), P("col", "row"), P("col", "row"))
    return jax.shard_map(
        local, mesh=mesh, in_specs=placed, out_specs=P("col", "row"), check_vma=False
    )
```

time: 197 us -> 114 us (0.58)
  the two profiles are of different devices: /device:TPU:315 before, /device:TPU:128 now
where the time goes in v1:
time: 114 us; the launch traced here: 113 us
  starting transfers between devices  47 us (41%)
  waiting for transfers between devices  42.1 us (37%)
  Pallas kernels  20.5 us (18%)
  local copies, waits for them, and re-layouts  3.81 us (3%)
    ppermute x6, starting transfers between devices, shifted(): lax.ppermute(block, axis, [((i + distance) % size, i) for i in range(size)])  47 us
    ppermute x6, waiting for transfers between devices, shifted(): lax.ppermute(block, axis, [((i + distance) % size, i) for i in range(size)])  42.1 us
    pallas_call x4, Pallas kernels, multiply(): pl.pallas_call(kernel, out_shape=jax.ShapeDtypeStruct((side, side), kind)...  18.9 us
    unnamed x8, local copies, waits for them, and re-layouts  3.81 us
  transfers between devices with their start and end apart: 6, of which 2 were waited for; matrix products, arithmetic and copies ran while one was open for 0% of the time, Pallas kernels for 12%

profile of v1, /device:TPU:128, one launch (start us, length us, event | category | flops | bytes accessed | tf_op | source)
XLA Modules:
  0.0 113.5 jit_solution(2110331661137261193)
XLA Ops:
  0.0 0.0 copy-start
  0.0 1.2 %copy-done = bf16[1024,512]{1,0:T(8,128)(2,1)S(1)} copy-done((bf16[1024,512]{1,0:T(8,128)(2,1)S(1)}, bf16[1024,512]{1,0:T(8,128)(2,1)}, u32[]{:S(2)}) %copy-start) | copy-done | bytes 1048600
  1.2 0.0 copy-start.1
  1.2 1.2 %copy-done.1 = bf16[512,1024]{1,0:T(8,128)(2,1)S(1)} copy-done((bf16[512,1024]{1,0:T(8,128)(2,1)S(1)}, bf16[512,1024]{1,0:T(8,128)(2,1)}, u32[]{:S(2)}) %copy-start.1) | copy-done | bytes 1048600
  2.5 0.0 copy-start.2
  2.5 0.7 copy-done.2
  3.1 0.0 copy-start.3
  3.1 0.7 copy-done.3
  3.8 1.5 %pack.1 = (bf16[1552,128]{1,0:T(8,128)(2,1)S(1)}, bf16[1552,128]{1,0:T(8,128)(2,1)S(1)}) custom-call(s32[4,8]{1,0:T(4,128)S(1)} %bitcast.1, s32[4,8]{1,0:T(4,128)S(1)} %copy-done.3, bf16[1024,512]{1,0:T(8,128)(2,1)S(1)} %copy-done, bf16[512,1024]{1,0:T(8,128)(2,1)S(1)} %copy-done.1), custom_call_target="tpu_custom_call" | custom-call | bytes 2097152 | tf_op jit(solution)/shard_map/pack/pallas_call | solution.py:69
  5.3 1.9 %collective-permute-start = (bf16[1552,128]{1,0:T(8,128)(2,1)S(1)}, bf16[1552,128]{1,0:T(8,128)(2,1)S(1)}, u32[]{:S(2)}, u32[]{:S(2)}) collective-permute-start(bf16[1552,128]{1,0:T(8,128)(2,1)S(1)} %get-tuple-element.7.refs_0_), channel_id=1, source_target_pairs={{32,0},{64,32},{96,64},{128,96},{160,128},{192,160},{224,192},{256... | collective-permute-start | bytes 1191944 | tf_op jit(solution)/shard_map/ppermute | solution.py:143
  7.3 16.6 %collective-permute-start.1 = (bf16[1552,128]{1,0:T(8,128)(2,1)S(1)}, bf16[1552,128]{1,0:T(8,128)(2,1)S(1)}, u32[]{:S(2)}, u32[]{:S(2)}) collective-permute-start(bf16[1552,128]{1,0:T(8,128)(2,1)S(1)} %get-tuple-element.8.refs_1_), channel_id=1, source_target_pairs={{1,0},{2,1},{3,2},{4,3},{5,4},{6,5},{7,6},{8,7},{9,8},{10,9},{11,1... | collective-permute-start | bytes 1191944 | tf_op jit(solution)/shard_map/ppermute | solution.py:143
  23.8 0.0 collective-permute-done.refs_1_
  23.8 1.9 %collective-permute-start.2 = (bf16[1552,128]{1,0:T(8,128)(2,1)S(1)}, bf16[1552,128]{1,0:T(8,128)(2,1)S(1)}, u32[]{:S(2)}, u32[]{:S(2)}) collective-permute-start(bf16[1552,128]{1,0:T(8,128)(2,1)S(1)} %collective-permute-done.refs_1_), channel_id=1, source_target_pairs={{32,0},{64,32},{96,64},{128,96},{160,128},{192,160},{224,192},{256... | collective-permute-start | bytes 1191944 | tf_op jit(solution)/shard_map/ppermute | solution.py:143
  25.8 21.8 %collective-permute-done.1.refs_2_ = bf16[1552,128]{1,0:T(8,128)(2,1)S(1)} collective-permute-done((bf16[1552,128]{1,0:T(8,128)(2,1)S(1)}, bf16[1552,128]{1,0:T(8,128)(2,1)S(1)}, u32[]{:S(2)}, u32[]{:S(2)}) %collective-permute-start.1) | collective-permute-done | bytes 397344 | tf_op jit(solution)/shard_map/ppermute | solution.py:143
  47.6 12.4 %collective-permute-start.3 = (bf16[1552,128]{1,0:T(8,128)(2,1)S(1)}, bf16[1552,128]{1,0:T(8,128)(2,1)S(1)}, u32[]{:S(2)}, u32[]{:S(2)}) collective-permute-start(bf16[1552,128]{1,0:T(8,128)(2,1)S(1)} %collective-permute-done.1.refs_2_), channel_id=1, source_target_pairs={{1,0},{2,1},{3,2},{4,3},{5,4},{6,5},{7,6},{8,7},{9,8},{10,9},{11,1... | collective-permute-start | bytes 1191944 | tf_op jit(solution)/shard_map/ppermute | solution.py:143
  60.0 0.0 collective-permute-done.2.refs_1_
  60.0 1.9 %collective-permute-start.4 = (bf16[1552,128]{1,0:T(8,128)(2,1)S(1)}, bf16[1552,128]{1,0:T(8,128)(2,1)S(1)}, u32[]{:S(2)}, u32[]{:S(2)}) collective-permute-start(bf16[1552,128]{1,0:T(8,128)(2,1)S(1)} %collective-permute-done.2.refs_1_), channel_id=1, source_target_pairs={{32,0},{64,32},{96,64},{128,96},{160,128},{192,160},{224,192},{256... | collective-permute-start | bytes 1191944 | tf_op jit(solution)/shard_map/ppermute | solution.py:143
  61.9 20.3 %collective-permute-done.3.refs_2_ = bf16[1552,128]{1,0:T(8,128)(2,1)S(1)} collective-permute-done((bf16[1552,128]{1,0:T(8,128)(2,1)S(1)}, bf16[1552,128]{1,0:T(8,128)(2,1)S(1)}, u32[]{:S(2)}, u32[]{:S(2)}) %collective-permute-start.3) | collective-permute-done | bytes 397344 | tf_op jit(solution)/shard_map/ppermute | solution.py:143
  82.2 12.3 %collective-permute-start.5 = (bf16[1552,128]{1,0:T(8,128)(2,1)S(1)}, bf16[1552,128]{1,0:T(8,128)(2,1)S(1)}, u32[]{:S(2)}, u32[]{:S(2)}) collective-permute-start(bf16[1552,128]{1,0:T(8,128)(2,1)S(1)} %collective-permute-done.3.refs_2_), channel_id=1, source_target_pairs={{1,0},{2,1},{3,2},{4,3},{5,4},{6,5},{7,6},{8,7},{9,8},{10,9},{11,1... | collective-permute-start | bytes 1191944 | tf_op jit(solution)/shard_map/ppermute | solution.py:143
  94.5 4.4 %multiply.4.refs_0_ = f32[1024,1024]{1,0:T(8,128)S(1)} custom-call(bf16[1552,128]{1,0:T(8,128)(2,1)S(1)} %get-tuple-element.7.refs_0_, bf16[1552,128]{1,0:T(8,128)(2,1)S(1)} %get-tuple-element.8.refs_1_), custom_call_target="tpu_custom_call" | custom-call | flops 1073741824 | bytes 2097152 | tf_op jit(solution)/shard_map/multiply/pallas_call | solution.py:124
  98.9 4.4 %multiply.5.refs_0_ = f32[1024,1024]{1,0:T(8,128)S(1)} custom-call(f32[1024,1024]{1,0:T(8,128)S(1)} %multiply.4.refs_0_, bf16[1552,128]{1,0:T(8,128)(2,1)S(1)} %collective-permute-done.refs_1_, bf16[1552,128]{1,0:T(8,128)(2,1)S(1)} %collective-permute-done.1.refs_2_), custom_call_target="tpu_custom_call" | custom-call | flops 1073741824 | bytes 2097152 | tf_op jit(solution)/shard_map/multiply/pallas_call | solution.py:124
  103.3 4.4 %multiply.6.refs_0_ = f32[1024,1024]{1,0:T(8,128)S(1)} custom-call(f32[1024,1024]{1,0:T(8,128)S(1)} %multiply.5.refs_0_, bf16[1552,128]{1,0:T(8,128)(2,1)S(1)} %collective-permute-done.2.refs_1_, bf16[1552,128]{1,0:T(8,128)(2,1)S(1)} %collective-permute-done.3.refs_2_), custom_call_target="tpu_custom_call" | custom-call | flops 1073741824 | bytes 2097152 | tf_op jit(solution)/shard_map/multiply/pallas_call | solution.py:124
  107.7 0.0 collective-permute-done.4.refs_1_
  107.7 0.0 collective-permute-done.5.refs_2_
  107.7 5.7 %multiply.7 = bf16[1024,1024]{1,0:T(8,128)(2,1)} custom-call(f32[1024,1024]{1,0:T(8,128)S(1)} %multiply.6.refs_0_, bf16[1552,128]{1,0:T(8,128)(2,1)S(1)} %collective-permute-done.4.refs_1_, bf16[1552,128]{1,0:T(8,128)(2,1)S(1)} %collective-permute-done.5.refs_2_), custom_call_target="tpu_custom_call" | custom-call | flops 1073741824 | bytes 2097152 | tf_op jit(solution)/shard_map/multiply/pallas_call | solution.py:124
Async XLA Ops:
  0.0 1.2 %copy-start = (bf16[1024,512]{1,0:T(8,128)(2,1)S(1)}, bf16[1024,512]{1,0:T(8,128)(2,1)}, u32[]{:S(2)}) copy-start(bf16[1024,512]{1,0:T(8,128)(2,1)} %left.1) | copy-start | bytes 3145732
  1.2 1.2 %copy-start.1 = (bf16[512,1024]{1,0:T(8,128)(2,1)S(1)}, bf16[512,1024]{1,0:T(8,128)(2,1)}, u32[]{:S(2)}) copy-start(bf16[512,1024]{1,0:T(8,128)(2,1)} %right.1) | copy-start | bytes 3145732
  2.5 0.7 copy-start.2
  3.1 0.7 copy-start.3
  5.3 18.5 %collective-permute-start = (bf16[1552,128]{1,0:T(8,128)(2,1)S(1)}, bf16[1552,128]{1,0:T(8,128)(2,1)S(1)}, u32[]{:S(2)}, u32[]{:S(2)}) collective-permute-start(bf16[1552,128]{1,0:T(8,128)(2,1)S(1)} %get-tuple-element.7.refs_0_), channel_id=1, source_target_pairs={{32,0},{64,32},{96,64},{128,96},{160,128},{192,160},{224,192},{256... | collective-permute-start | bytes 1191944 | tf_op jit(solution)/shard_map/ppermute | solution.py:143
  7.3 40.3 %collective-permute-start.1 = (bf16[1552,128]{1,0:T(8,128)(2,1)S(1)}, bf16[1552,128]{1,0:T(8,128)(2,1)S(1)}, u32[]{:S(2)}, u32[]{:S(2)}) collective-permute-start(bf16[1552,128]{1,0:T(8,128)(2,1)S(1)} %get-tuple-element.8.refs_1_), channel_id=1, source_target_pairs={{1,0},{2,1},{3,2},{4,3},{5,4},{6,5},{7,6},{8,7},{9,8},{10,9},{11,1... | collective-permute-start | bytes 1191944 | tf_op jit(solution)/shard_map/ppermute | solution.py:143
  23.8 36.2 %collective-permute-start.2 = (bf16[1552,128]{1,0:T(8,128)(2,1)S(1)}, bf16[1552,128]{1,0:T(8,128)(2,1)S(1)}, u32[]{:S(2)}, u32[]{:S(2)}) collective-permute-start(bf16[1552,128]{1,0:T(8,128)(2,1)S(1)} %collective-permute-done.refs_1_), channel_id=1, source_target_pairs={{32,0},{64,32},{96,64},{128,96},{160,128},{192,160},{224,192},{256... | collective-permute-start | bytes 1191944 | tf_op jit(solution)/shard_map/ppermute | solution.py:143
  47.6 34.7 %collective-permute-start.3 = (bf16[1552,128]{1,0:T(8,128)(2,1)S(1)}, bf16[1552,128]{1,0:T(8,128)(2,1)S(1)}, u32[]{:S(2)}, u32[]{:S(2)}) collective-permute-start(bf16[1552,128]{1,0:T(8,128)(2,1)S(1)} %collective-permute-done.1.refs_2_), channel_id=1, source_target_pairs={{1,0},{2,1},{3,2},{4,3},{5,4},{6,5},{7,6},{8,7},{9,8},{10,9},{11,1... | collective-permute-start | bytes 1191944 | tf_op jit(solution)/shard_map/ppermute | solution.py:143
  60.0 47.7 %collective-permute-start.4 = (bf16[1552,128]{1,0:T(8,128)(2,1)S(1)}, bf16[1552,128]{1,0:T(8,128)(2,1)S(1)}, u32[]{:S(2)}, u32[]{:S(2)}) collective-permute-start(bf16[1552,128]{1,0:T(8,128)(2,1)S(1)} %collective-permute-done.2.refs_1_), channel_id=1, source_target_pairs={{32,0},{64,32},{96,64},{128,96},{160,128},{192,160},{224,192},{256... | collective-permute-start | bytes 1191944 | tf_op jit(solution)/shard_map/ppermute | solution.py:143
  82.2 25.5 %collective-permute-start.5 = (bf16[1552,128]{1,0:T(8,128)(2,1)S(1)}, bf16[1552,128]{1,0:T(8,128)(2,1)S(1)}, u32[]{:S(2)}, u32[]{:S(2)}) collective-permute-start(bf16[1552,128]{1,0:T(8,128)(2,1)S(1)} %collective-permute-done.3.refs_2_), channel_id=1, source_target_pairs={{1,0},{2,1},{3,2},{4,3},{5,4},{6,5},{7,6},{8,7},{9,8},{10,9},{11,1... | collective-permute-start | bytes 1191944 | tf_op jit(solution)/shard_map/ppermute | solution.py:143

commit v2 on v0

v2 whole, which is shorter than its diff:
```python
import jax
import jax.numpy as jnp
from jax import lax
from jax.experimental import pallas as pl
from jax.experimental.pallas import tpu as pltpu
from jax.sharding import PartitionSpec as P

TILE = 128
TB = 8
KT = 4
OCC = 12
HEAD = 16
PACK = OCC * TILE + HEAD
CUT = OCC // 2 * TILE
EMPTY = 64.0
SIDE = TB * TILE
DEPTH = KT * TILE
BLOCK = 256
VMEM_LIMIT = 20 * 1024 * 1024
PACK_VMEM = 60 * 1024 * 1024
VMEM = pl.BlockSpec(memory_space=pltpu.VMEM)
SMEM = pl.BlockSpec(memory_space=pltpu.SMEM)
HBM = pl.BlockSpec(memory_space=pltpu.HBM)
COST = pl.CostEstimate(flops=1, bytes_accessed=1, transcendentals=0)

X, Y, Z = 4, 8, 12
RUN = 6
HALF_LOOP = 16
N_COL = 32


def device(x, y, z, core):
    z = z % Z
    return (x * RUN + z % RUN) * N_COL + (z // RUN) * HALF_LOOP + (y % Y) * 2 + core


def per_line(*routes):
    return [
        (device(x, y, z, core), device(x, to_y, z + dz, to_core))
        for x in range(X)
        for z in range(Z)
        for (y, core), (to_y, to_core), dz in routes
    ]


def over(source, target):
    (from_dx, from_z), (to_dx, to_z) = source, target
    return [
        (((x + from_dx) % X * RUN + from_z) * N_COL + c, ((x + to_dx) % X * RUN + to_z) * N_COL + c)
        for x in range(X)
        for c in range(N_COL)
    ]


def down(top):
    return [pair for z in range(top) for pair in over((0, z + 1), (0, z))]


def right_hop(distance, within):
    return [
        (q * N_COL + half * HALF_LOOP + c + distance, q * N_COL + half * HALF_LOOP + c)
        for q in range(X * RUN)
        for half in range(2)
        for c in range(within - distance)
    ]


def send(block, route):
    return lax.ppermute(block, ("row", "col"), route)


def after(block, *others):
    return lax.optimization_barrier((block, *others))[0]


def number_slots(mask_at, tile_rows, tile_cols, slots):
    for j in range(OCC):
        slots[j] = 0
    count = jnp.int32(0)
    for i in range(tile_rows):
        for k in range(tile_cols):
            occupied = mask_at(i, k) != 0

            @pl.when(occupied & (count < OCC))
            def _():
                slots[count] = i * tile_cols + k

            count = count + occupied.astype(jnp.int32)
    return jnp.minimum(count, OCC)


def tile_at(tile, tile_cols):
    i = pl.multiple_of(tile // tile_cols * TILE, TILE)
    k = pl.multiple_of(tile % tile_cols * TILE, TILE)
    return pl.ds(i, TILE), pl.ds(k, TILE)


def gather_tiles(source, slots, count, tile_cols, outs):
    lane = lax.broadcasted_iota(jnp.int32, (HEAD, TILE), 1)
    head = jnp.full((HEAD, TILE), EMPTY, jnp.float32)
    for j in range(OCC):
        tile = slots[j]
        data = source[tile_at(tile, tile_cols)]
        for out, base in outs:
            at = j * TILE - base
            if 0 <= at <= out.shape[0] - TILE:
                out[at : at + TILE, :] = data
        head = jnp.where((lane == j) & (j < count), tile.astype(jnp.float32), head)
    for out, base in outs:
        if base + out.shape[0] == PACK:
            out[out.shape[0] - HEAD :, :] = head.astype(jnp.bfloat16)


def pack_kernel(left_mask_across, right_mask, left, right, *refs):
    left_a, left_b, left_all, right_all, left_here, right_here, slots, sems = refs
    left_copy = pltpu.make_async_copy(left, left_here, sems.at[0])
    right_copy = pltpu.make_async_copy(right, right_here, sems.at[1])
    left_copy.start()
    right_copy.start()
    left_count = number_slots(lambda i, k: left_mask_across[k, i], TB, KT, slots.at[0])
    right_count = number_slots(lambda i, k: right_mask[i, k], KT, TB, slots.at[1])
    left_copy.wait()
    gather_tiles(left_here, slots.at[0], left_count, KT, [(left_a, 0), (left_b, CUT), (left_all, 0)])
    right_copy.wait()
    gather_tiles(right_here, slots.at[1], right_count, TB, [(right_all, 0)])


def pack(left_mask, right_mask, left, right):
    return pl.pallas_call(
        pack_kernel,
        out_shape=tuple(jax.ShapeDtypeStruct((n, TILE), jnp.bfloat16) for n in (CUT, PACK - CUT, PACK, PACK)),
        in_specs=[SMEM, SMEM, HBM, HBM],
        out_specs=(VMEM,) * 4,
        scratch_shapes=[
            pltpu.VMEM((SIDE, DEPTH), jnp.bfloat16),
            pltpu.VMEM((DEPTH, SIDE), jnp.bfloat16),
            pltpu.SMEM((2, OCC), jnp.int32),
            pltpu.SemaphoreType.DMA((2,)),
        ],
        compiler_params=pltpu.CompilerParams(vmem_limit_bytes=PACK_VMEM),
        cost_estimate=COST,
        name="pack",
    )(left_mask.T, right_mask, left, right)


def one_of(value, members):
    found = value < 0
    for member in members:
        found = found | (value == member)
    return found


def places_of(choice, wanted):
    z = lax.axis_index("row") % RUN
    c = lax.axis_index("col") % HALF_LOOP
    here = z < 0
    at_c = {at: tuple(k for k in range(HALF_LOOP) if choice[at, k] in wanted) for at in range(RUN)}
    for members in sorted(set(at_c.values())):
        if members:
            rows = one_of(z, [at for at in range(RUN) if at_c[at] == members])
            here = here | (rows if len(members) == HALF_LOOP else rows & one_of(c, members))
    return here


def pick(choice, pieces, use):
    for n, piece in enumerate(pieces):

        @pl.when(places_of(choice, {n}))
        def _(piece=piece):
            use(piece)


def whole(array):
    return ((array, 0), (array, CUT))


def halves(first, second):
    return ((first, 0), (second, 0))


def choose(of):
    arrays, pieces, choice = [], [], {}

    def number(array):
        known = [n for n, other in enumerate(arrays) if other is array]
        if not known:
            arrays.append(array)
        return known[0] if known else len(arrays) - 1

    for z in range(RUN):
        for c in range(HALF_LOOP):
            piece = of(z, c)
            if piece is None:
                choice[z, c] = None
                continue
            piece = tuple((number(array), base) for array, base in piece)
            if piece not in pieces:
                pieces.append(piece)
            choice[z, c] = pieces.index(piece)
    return arrays, pieces, choice


def rows_of(piece, first, n):
    ref, base = piece[first >= CUT]
    first = first - CUT * (first >= CUT) + base
    return ref[first : first + n, :]


def spread_all(work, heads, numbers, sem):
    for n, (choice, refs, _, _) in enumerate(work):

        def read(packed, n=n):
            heads[n] = rows_of(packed, OCC * TILE, HEAD).astype(jnp.float32).astype(jnp.int32)[:8]

        pick(choice, refs, read)
    copy = pltpu.make_async_copy(heads, numbers, sem)
    copy.start()
    for choice, _, dense, _ in work:

        @pl.when(jnp.logical_not(places_of(choice, {None})))
        def _(dense=dense):
            dense[...] = jnp.zeros_like(dense)

    copy.wait()
    for n, (choice, refs, dense, tile_cols) in enumerate(work):

        def place(packed, n=n, dense=dense, tile_cols=tile_cols):
            for j in range(OCC):
                tile = numbers[n, 0, j]

                @pl.when(tile < TB * KT)
                def _():
                    dense[tile_at(tile, tile_cols)] = rows_of(packed, j * TILE, TILE)

        pick(choice, refs, place)


def head_scratch(n):
    return [
        pltpu.VMEM((n, 8, TILE), jnp.int32),
        pltpu.SMEM((n, 8, TILE), jnp.int32),
        pltpu.SemaphoreType.DMA(()),
    ]


def take(refs, n):
    return [refs.pop(0) for _ in range(n)]


def take_pieces(refs, chosen):
    arrays, pieces, _ = chosen
    here = take(refs, len(arrays))
    return [tuple((here[n], base) for n, base in piece) for piece in pieces]


def multiply(total, steps, last):
    first, n = total is None, len(steps)
    skips = [step[0][2] for step in steps]
    sometimes = [at for at in range(n) if None in skips[at].values()]
    always = n - len(sometimes)
    assert sometimes == list(range(always, n))

    def kernel(*refs):
        refs = list(refs)
        before = None if first else refs.pop(0)
        inputs = [(take_pieces(refs, left), take_pieces(refs, right)) for left, right in steps]
        out, left, right, heads, numbers, sem = take(refs, 6)
        work = []
        for at, (left_in, right_in) in enumerate(inputs):
            inner = pl.ds(at * DEPTH, DEPTH)
            work.append((steps[at][0][2], left_in, left.at[:, inner], KT))
            work.append((steps[at][1][2], right_in, right.at[inner, :], TB))
        spread_all(work, heads, numbers, sem)
        rounded, sems = refs if last else (None, None)

        def add_up(rows, depth, then):
            part = jnp.dot(left[rows, :depth], right[:depth, :], preferred_element_type=jnp.float32)
            then(rows, part if first else before[rows, :] + part)

        def each_block(depth, then):
            for block in range(SIDE // BLOCK):
                add_up(pl.ds(block * BLOCK, BLOCK), depth, then)

        def keep(rows, value):
            out[rows, :] = value

        def write(rows, value):
            at = rows.start // BLOCK
            rounded[rows, :] = value.astype(jnp.bfloat16)
            pltpu.make_async_copy(rounded.at[rows, :], out.at[rows, :], sems.at[at]).start()

        then = write if last else keep
        if sometimes:
            skipped = places_of(skips[always], {None})

            @pl.when(skipped)
            def _():
                each_block(always * DEPTH, then)

            @pl.when(jnp.logical_not(skipped))
            def _():
                each_block(n * DEPTH, then)

        else:
            each_block(n * DEPTH, then)
        if last:
            for block in range(SIDE // BLOCK):
                rows = pl.ds(block * BLOCK, BLOCK)
                pltpu.make_async_copy(rounded.at[rows, :], out.at[rows, :], sems.at[block]).wait()

    args = [] if first else [total]
    for left, right in steps:
        args += left[0] + right[0]
    scratch = [
        pltpu.VMEM((SIDE, n * DEPTH), jnp.bfloat16),
        pltpu.VMEM((n * DEPTH, SIDE), jnp.bfloat16),
    ] + head_scratch(2 * n)
    if last:
        scratch += [
            pltpu.VMEM((SIDE, SIDE), jnp.bfloat16),
            pltpu.SemaphoreType.DMA((SIDE // BLOCK,)),
        ]
    return pl.pallas_call(
        kernel,
        out_shape=jax.ShapeDtypeStruct((SIDE, SIDE), jnp.bfloat16 if last else jnp.float32),
        in_specs=[VMEM] * len(args),
        out_specs=HBM if last else VMEM,
        scratch_shapes=scratch,
        compiler_params=pltpu.CompilerParams(vmem_limit_bytes=VMEM_LIMIT),
        cost_estimate=COST,
        name="finish" if last else "multiply",
    )(*args)


def local(left_factor, left_mask, right_factor, right_mask):
    la, lb, l0, r0 = pack(left_mask, right_mask, left_factor, right_factor)

    ring = down(5) + over((1, 0), (0, 5))
    first_a, first_b = send(la, ring), send(lb, ring)
    over_both = send(l0, over((1, 1), (0, 5)) + over((1, 2), (0, 4)))
    second_a, second_b = send(first_a, down(5)), send(first_b, down(5))
    moved = send(r0, per_line(((0, 1), (7, 1), 0), ((0, 0), (0, 1), 0), ((1, 0), (1, 1), 0)))
    crossed = send(moved, per_line(((0, 1), (7, 0), 6), ((7, 1), (7, 1), 6), ((1, 1), (6, 0), 6)))
    n1 = send(r0, right_hop(1, 16))
    n2 = send(r0, right_hop(2, 16))
    n3 = send(n2, right_hop(1, 14))

    def early(c):
        return c < 15

    lefts = {
        1: [halves(first_a, first_b)] * 6,
        2: [halves(second_a, second_b)] * 5 + [whole(over_both)],
    }
    total = multiply(
        None,
        [
            (choose(lambda z, c: whole(l0)), choose(lambda z, c: whole(r0))),
            (
                choose(lambda z, c: lefts[1][z] if early(c) else None),
                choose(lambda z, c: whole(n1) if early(c) else None),
            ),
        ],
        False,
    )
    third = send(after(jnp.concatenate([second_a, second_b]), over_both), down(4))
    changed = send(over_both, over((0, 5), (0, 4)) + over((0, 4), (0, 5)))
    lefts[3] = [whole(third)] * 4 + [whole(changed)] * 2
    crossed_late = after(crossed, over_both)
    g1 = send(crossed_late, per_line(((7, 0), (7, 1), 0)))
    g2 = send(crossed_late, per_line(((7, 0), (6, 1), 0), ((7, 1), (7, 0), 0), ((6, 0), (7, 1), 0)))

    def right_of(step, c):
        return whole({1: (n1, g1), 2: (n2, crossed), 3: (n3, g2)}[step][c + step >= HALF_LOOP])

    steps = [
        (choose(lambda z, c: lefts[step][z]), choose(lambda z, c: right_of(step, c))) for step in (2, 3)
    ]
    steps.append(
        (
            choose(lambda z, c: None if early(c) else lefts[1][z]),
            choose(lambda z, c: None if early(c) else right_of(1, c)),
        )
    )
    return multiply(total, steps, True)


def solution(mesh):
    placed = (P("col", "row"), P("col", "row"), P("col", "row"), P("col", "row"))
    return jax.shard_map(
        local, mesh=mesh, in_specs=placed, out_specs=P("col", "row"), check_vma=False
    )
```

time: 197 us -> 85.8 us (0.44)
  the two profiles are of different devices: /device:TPU:315 before, /device:TPU:185 now
where the time goes in v2:
time: 85.8 us; the launch traced here: 85.3 us
  starting transfers between devices  47.2 us (55%)
  waiting for transfers between devices  23.5 us (27%)
  Pallas kernels  12.1 us (14%)
  local copies, waits for them, and re-layouts  1.99 us (2%)
    ppermute x14, starting transfers between devices, send(): return lax.ppermute(block, ('row', 'col'), route)  47.2 us
    ppermute x14, waiting for transfers between devices, send(): return lax.ppermute(block, ('row', 'col'), route)  23.5 us
    pallas_call x2, Pallas kernels, multiply(): pl.pallas_call(kernel, out_shape=jax.ShapeDtypeStruct((SIDE, SIDE), jnp.b...  8.74 us
    pallas_call x1, Pallas kernels, pack(): pl.pallas_call(pack_kernel, out_shape=tuple((jax.ShapeDtypeStruct((n, TIL...  3.4 us
    unnamed x4, local copies, waits for them, and re-layouts  1.99 us
  transfers between devices with their start and end apart: 14, of which 3 were waited for; matrix products, arithmetic and copies ran while one was open for 0% of the time, Pallas kernels for 3%

profile of v2, /device:TPU:185, one launch (start us, length us, event | category | flops | bytes accessed | tf_op | source)
XLA Modules:
  0.0 85.3 jit_solution(3975594651862105391)
XLA Ops:
  0.0 3.4 %pack.1 = (bf16[768,128]{1,0:T(8,128)(2,1)}, bf16[784,128]{1,0:T(8,128)(2,1)}, bf16[1552,128]{1,0:T(8,128)(2,1)}, bf16[1552,128]{1,0:T(8,128)(2,1)}) custom-call(s32[4,8]{1,0:T(4,128)} %bitcast.1, s32[4,8]{1,0:T(4,128)} %right_mask.1, bf16[1024,512]{1,0:T(8,128)(2,1)} %left.1, bf16[512,1024]{1,0:T(8,128)(2,1)} %right.1), custom_call_target="tpu_custom_call" | custom-call | flops 1 | bytes 1 | tf_op jit(solution)/shard_map/pack/pallas_call | solution.py:129
  3.4 1.3 %collective-permute-start.7 = (bf16[1552,128]{1,0:T(8,128)(2,1)}, bf16[1552,128]{1,0:T(8,128)(2,1)S(1)}, u32[]{:S(2)}, u32[]{:S(2)}) collective-permute-start(bf16[1552,128]{1,0:T(8,128)(2,1)} %get-tuple-element.12.refs_1_), channel_id=1, source_target_pairs={{1,15},{0,1},{2,3},{33,47},{32,33},{34,35},{65,79},{64,65},{66,67}... | collective-permute-start | bytes 1191944 | tf_op jit(solution)/shard_map/ppermute | solution.py:69
  4.7 1.9 %collective-permute-start = (bf16[768,128]{1,0:T(8,128)(2,1)}, bf16[768,128]{1,0:T(8,128)(2,1)S(1)}, u32[]{:S(2)}, u32[]{:S(2)}) collective-permute-start(bf16[768,128]{1,0:T(8,128)(2,1)} %get-tuple-element.13), channel_id=1, source_target_pairs={{32,0},{33,1},{34,2},{35,3},{36,4},{37,5},{38,6},{39,7},{40,8},{41... | collective-permute-start | bytes 589832 | tf_op jit(solution)/shard_map/ppermute | solution.py:69
  6.6 1.9 %collective-permute-start.1 = (bf16[784,128]{1,0:T(8,128)(2,1)}, bf16[784,128]{1,0:T(8,128)(2,1)S(1)}, u32[]{:S(2)}, u32[]{:S(2)}) collective-permute-start(bf16[784,128]{1,0:T(8,128)(2,1)} %get-tuple-element.14), channel_id=1, source_target_pairs={{32,0},{33,1},{34,2},{35,3},{36,4},{37,5},{38,6},{39,7},{40,8},{41... | collective-permute-start | bytes 602120 | tf_op jit(solution)/shard_map/ppermute | solution.py:69
  8.6 9.2 %collective-permute-start.5 = (bf16[1552,128]{1,0:T(8,128)(2,1)}, bf16[1552,128]{1,0:T(8,128)(2,1)S(1)}, u32[]{:S(2)}, u32[]{:S(2)}) collective-permute-start(bf16[1552,128]{1,0:T(8,128)(2,1)} %get-tuple-element.11.refs_0_), channel_id=1, source_target_pairs={{224,160},{225,161},{226,162},{227,163},{228,164},{229,165},{230,1... | collective-permute-start | bytes 1191944 | tf_op jit(solution)/shard_map/ppermute | solution.py:69
  17.8 2.4 %collective-permute-start.6 = (bf16[1552,128]{1,0:T(8,128)(2,1)}, bf16[1552,128]{1,0:T(8,128)(2,1)S(1)}, u32[]{:S(2)}, u32[]{:S(2)}) collective-permute-start(bf16[1552,128]{1,0:T(8,128)(2,1)} %get-tuple-element.12.refs_1_), channel_id=1, source_target_pairs={{2,0},{3,1},{4,2},{5,3},{6,4},{7,5},{8,6},{9,7},{10,8},{11,9},{12,... | collective-permute-start | bytes 1191944 | tf_op jit(solution)/shard_map/ppermute | solution.py:69
  20.2 0.0 collective-permute-done.refs_2_.refs_10_
  20.2 5.4 %collective-permute-start.3 = (bf16[768,128]{1,0:T(8,128)(2,1)S(1)}, bf16[768,128]{1,0:T(8,128)(2,1)S(1)}, u32[]{:S(2)}, u32[]{:S(2)}) collective-permute-start(bf16[768,128]{1,0:T(8,128)(2,1)S(1)} %collective-permute-done.refs_2_.refs_10_), channel_id=1, source_target_pairs={{32,0},{33,1},{34,2},{35,3},{36,4},{37,5},{38,6},{39,7},{40,8},{41... | collective-permute-start | bytes 589832 | tf_op jit(solution)/shard_map/ppermute | solution.py:69
  25.7 0.0 collective-permute-done.1.refs_3_.refs_11_
  25.7 1.9 %collective-permute-start.4 = (bf16[784,128]{1,0:T(8,128)(2,1)S(1)}, bf16[784,128]{1,0:T(8,128)(2,1)S(1)}, u32[]{:S(2)}, u32[]{:S(2)}) collective-permute-start(bf16[784,128]{1,0:T(8,128)(2,1)S(1)} %collective-permute-done.1.refs_3_.refs_11_), channel_id=1, source_target_pairs={{32,0},{33,1},{34,2},{35,3},{36,4},{37,5},{38,6},{39,7},{40,8},{41... | collective-permute-start | bytes 602120 | tf_op jit(solution)/shard_map/ppermute | solution.py:69
  27.6 0.0 collective-permute-done.7
  27.6 9.8 %collective-permute-start.8 = (bf16[1552,128]{1,0:T(8,128)(2,1)S(1)}, bf16[1552,128]{1,0:T(8,128)(2,1)S(1)}, u32[]{:S(2)}, u32[]{:S(2)}) collective-permute-start(bf16[1552,128]{1,0:T(8,128)(2,1)S(1)} %collective-permute-done.7), channel_id=1, source_target_pairs={{1,30},{15,31},{3,28},{33,62},{47,63},{35,60},{65,94},{79,95},{67,... | collective-permute-start | bytes 1191944 | tf_op jit(solution)/shard_map/ppermute | solution.py:69
  37.4 0.0 collective-permute-done.3.refs_1_
  37.4 1.3 %collective-permute-start.2 = (bf16[1552,128]{1,0:T(8,128)(2,1)}, bf16[1552,128]{1,0:T(8,128)(2,1)S(1)}, u32[]{:S(2)}, u32[]{:S(2)}) collective-permute-start(bf16[1552,128]{1,0:T(8,128)(2,1)} %get-tuple-element.12.refs_1_), channel_id=1, source_target_pairs={{1,0},{2,1},{3,2},{4,3},{5,4},{6,5},{7,6},{8,7},{9,8},{10,9},{11,1... | collective-permute-start | bytes 1191944 | tf_op jit(solution)/shard_map/ppermute | solution.py:69
  38.7 13.6 %collective-permute-done.5.refs_3_ = bf16[1552,128]{1,0:T(8,128)(2,1)S(1)} collective-permute-done((bf16[1552,128]{1,0:T(8,128)(2,1)}, bf16[1552,128]{1,0:T(8,128)(2,1)S(1)}, u32[]{:S(2)}, u32[]{:S(2)}) %collective-permute-start.5) | collective-permute-done | bytes 397344 | tf_op jit(solution)/shard_map/ppermute | solution.py:69
  52.3 0.7 collective-permute-start.10
  53.0 0.0 collective-permute-done.6.refs_4_
  53.0 0.7 collective-permute-start.11
  53.7 0.0 collective-permute-done.4.refs_2_
  53.8 1.9 %collective-permute-start.9 = (bf16[1552,128]{1,0:T(8,128)(2,1)S(1)}, bf16[1552,128]{1,0:T(8,128)(2,1)S(1)}, u32[]{:S(2)}, u32[]{:S(2)}) collective-permute-start(bf16[1552,128]{1,0:T(8,128)(2,1)S(1)} %pad_maximum_fusion), channel_id=1, source_target_pairs={{32,0},{33,1},{34,2},{35,3},{36,4},{37,5},{38,6},{39,7},{40,8},{41... | collective-permute-start | bytes 1191944 | tf_op jit(solution)/shard_map/ppermute | solution.py:69
  55.7 9.4 %collective-permute-done.8.refs_5_ = bf16[1552,128]{1,0:T(8,128)(2,1)S(1)} collective-permute-done((bf16[1552,128]{1,0:T(8,128)(2,1)S(1)}, bf16[1552,128]{1,0:T(8,128)(2,1)S(1)}, u32[]{:S(2)}, u32[]{:S(2)}) %collective-permute-start.8) | collective-permute-done | bytes 397344 | tf_op jit(solution)/shard_map/ppermute | solution.py:69
  65.1 1.3 %collective-permute-start.13 = (bf16[1552,128]{1,0:T(8,128)(2,1)S(1)}, bf16[1552,128]{1,0:T(8,128)(2,1)S(1)}, u32[]{:S(2)}, u32[]{:S(2)}) collective-permute-start(bf16[1552,128]{1,0:T(8,128)(2,1)S(1)} %collective-permute-done.8.refs_5_), channel_id=1, source_target_pairs={{14,15},{46,47},{78,79},{110,111},{142,143},{174,175},{30,31},{62,... | collective-permute-start | bytes 1191944 | tf_op jit(solution)/shard_map/ppermute | solution.py:69
  66.4 0.0 collective-permute-done.2.refs_4_
  66.4 7.5 %collective-permute-start.12 = (bf16[1552,128]{1,0:T(8,128)(2,1)S(1)}, bf16[1552,128]{1,0:T(8,128)(2,1)S(1)}, u32[]{:S(2)}, u32[]{:S(2)}) collective-permute-start(bf16[1552,128]{1,0:T(8,128)(2,1)S(1)} %collective-permute-done.8.refs_5_), channel_id=1, source_target_pairs={{14,13},{15,14},{12,15},{46,45},{47,46},{44,47},{78,77},{79,78},{7... | collective-permute-start | bytes 1191944 | tf_op jit(solution)/shard_map/ppermute | solution.py:69
  73.9 0.0 copy-start
  73.9 1.0 %copy-done = bf16[1552,128]{1,0:T(8,128)(2,1)S(1)} copy-done((bf16[1552,128]{1,0:T(8,128)(2,1)S(1)}, bf16[1552,128]{1,0:T(8,128)(2,1)}, u32[]{:S(2)}) %copy-start) | copy-done | bytes 397336
  74.9 0.0 copy-start.1
  74.9 1.0 %copy-done.1 = bf16[1552,128]{1,0:T(8,128)(2,1)S(1)} copy-done((bf16[1552,128]{1,0:T(8,128)(2,1)S(1)}, bf16[1552,128]{1,0:T(8,128)(2,1)}, u32[]{:S(2)}) %copy-start.1) | copy-done | bytes 397336
  75.9 2.4 %multiply.1.refs_0_ = f32[1024,1024]{1,0:T(8,128)S(1)} custom-call(bf16[1552,128]{1,0:T(8,128)(2,1)S(1)} %copy-done, bf16[1552,128]{1,0:T(8,128)(2,1)S(1)} %copy-done.1, bf16[768,128]{1,0:T(8,128)(2,1)S(1)} %collective-permute-done.refs_2_.refs_10_, bf16[784,128]{1,0:T(8,128)(2,1)S(1)} %collective-permute-done.1.refs_3_.refs_11_, ...), custom_call_target="tpu_custom_call" | custom-call | flops 1 | bytes 1 | tf_op jit(solution)/shard_map/multiply/pallas_call | solution.py:323
  78.3 0.0 collective-permute-done.10.refs_7_
  78.4 0.0 collective-permute-done.11.refs_8_
  78.4 0.0 collective-permute-done.9.refs_6_
  78.4 0.0 collective-permute-done.13.refs_12_
  78.4 0.4 collective-permute-done.12.refs_9_
  78.8 6.3 %finish.1 = bf16[1024,1024]{1,0:T(8,128)(2,1)} custom-call(f32[1024,1024]{1,0:T(8,128)S(1)} %multiply.1.refs_0_, bf16[768,128]{1,0:T(8,128)(2,1)S(1)} %collective-permute-done.3.refs_1_, bf16[784,128]{1,0:T(8,128)(2,1)S(1)} %collective-permute-done.4.refs_2_, bf16[1552,128]{1,0:T(8,128)(2,1)S(1)} %collective-permute-done.5.refs_3_, ...), custom_call_target="tpu_custom_call" | custom-call | flops 1 | bytes 1 | tf_op jit(solution)/shard_map/finish/pallas_call | solution.py:323
  (1 shorter events, 0.0 us)
Async XLA Ops:
  3.4 24.2 %collective-permute-start.7 = (bf16[1552,128]{1,0:T(8,128)(2,1)}, bf16[1552,128]{1,0:T(8,128)(2,1)S(1)}, u32[]{:S(2)}, u32[]{:S(2)}) collective-permute-start(bf16[1552,128]{1,0:T(8,128)(2,1)} %get-tuple-element.12.refs_1_), channel_id=1, source_target_pairs={{1,15},{0,1},{2,3},{33,47},{32,33},{34,35},{65,79},{64,65},{66,67}... | collective-permute-start | bytes 1191944 | tf_op jit(solution)/shard_map/ppermute | solution.py:69
  4.7 15.5 %collective-permute-start = (bf16[768,128]{1,0:T(8,128)(2,1)}, bf16[768,128]{1,0:T(8,128)(2,1)S(1)}, u32[]{:S(2)}, u32[]{:S(2)}) collective-permute-start(bf16[768,128]{1,0:T(8,128)(2,1)} %get-tuple-element.13), channel_id=1, source_target_pairs={{32,0},{33,1},{34,2},{35,3},{36,4},{37,5},{38,6},{39,7},{40,8},{41... | collective-permute-start | bytes 589832 | tf_op jit(solution)/shard_map/ppermute | solution.py:69
  6.6 19.0 %collective-permute-start.1 = (bf16[784,128]{1,0:T(8,128)(2,1)}, bf16[784,128]{1,0:T(8,128)(2,1)S(1)}, u32[]{:S(2)}, u32[]{:S(2)}) collective-permute-start(bf16[784,128]{1,0:T(8,128)(2,1)} %get-tuple-element.14), channel_id=1, source_target_pairs={{32,0},{33,1},{34,2},{35,3},{36,4},{37,5},{38,6},{39,7},{40,8},{41... | collective-permute-start | bytes 602120 | tf_op jit(solution)/shard_map/ppermute | solution.py:69
  8.6 43.8 %collective-permute-start.5 = (bf16[1552,128]{1,0:T(8,128)(2,1)}, bf16[1552,128]{1,0:T(8,128)(2,1)S(1)}, u32[]{:S(2)}, u32[]{:S(2)}) collective-permute-start(bf16[1552,128]{1,0:T(8,128)(2,1)} %get-tuple-element.11.refs_0_), channel_id=1, source_target_pairs={{224,160},{225,161},{226,162},{227,163},{228,164},{229,165},{230,1... | collective-permute-start | bytes 1191944 | tf_op jit(solution)/shard_map/ppermute | solution.py:69
  17.8 35.2 %collective-permute-start.6 = (bf16[1552,128]{1,0:T(8,128)(2,1)}, bf16[1552,128]{1,0:T(8,128)(2,1)S(1)}, u32[]{:S(2)}, u32[]{:S(2)}) collective-permute-start(bf16[1552,128]{1,0:T(8,128)(2,1)} %get-tuple-element.12.refs_1_), channel_id=1, source_target_pairs={{2,0},{3,1},{4,2},{5,3},{6,4},{7,5},{8,6},{9,7},{10,8},{11,9},{12,... | collective-permute-start | bytes 1191944 | tf_op jit(solution)/shard_map/ppermute | solution.py:69
  20.2 17.2 %collective-permute-start.3 = (bf16[768,128]{1,0:T(8,128)(2,1)S(1)}, bf16[768,128]{1,0:T(8,128)(2,1)S(1)}, u32[]{:S(2)}, u32[]{:S(2)}) collective-permute-start(bf16[768,128]{1,0:T(8,128)(2,1)S(1)} %collective-permute-done.refs_2_.refs_10_), channel_id=1, source_target_pairs={{32,0},{33,1},{34,2},{35,3},{36,4},{37,5},{38,6},{39,7},{40,8},{41... | collective-permute-start | bytes 589832 | tf_op jit(solution)/shard_map/ppermute | solution.py:69
  25.7 28.1 %collective-permute-start.4 = (bf16[784,128]{1,0:T(8,128)(2,1)S(1)}, bf16[784,128]{1,0:T(8,128)(2,1)S(1)}, u32[]{:S(2)}, u32[]{:S(2)}) collective-permute-start(bf16[784,128]{1,0:T(8,128)(2,1)S(1)} %collective-permute-done.1.refs_3_.refs_11_), channel_id=1, source_target_pairs={{32,0},{33,1},{34,2},{35,3},{36,4},{37,5},{38,6},{39,7},{40,8},{41... | collective-permute-start | bytes 602120 | tf_op jit(solution)/shard_map/ppermute | solution.py:69
  27.6 37.5 %collective-permute-start.8 = (bf16[1552,128]{1,0:T(8,128)(2,1)S(1)}, bf16[1552,128]{1,0:T(8,128)(2,1)S(1)}, u32[]{:S(2)}, u32[]{:S(2)}) collective-permute-start(bf16[1552,128]{1,0:T(8,128)(2,1)S(1)} %collective-permute-done.7), channel_id=1, source_target_pairs={{1,30},{15,31},{3,28},{33,62},{47,63},{35,60},{65,94},{79,95},{67,... | collective-permute-start | bytes 1191944 | tf_op jit(solution)/shard_map/ppermute | solution.py:69
  37.4 29.0 %collective-permute-start.2 = (bf16[1552,128]{1,0:T(8,128)(2,1)}, bf16[1552,128]{1,0:T(8,128)(2,1)S(1)}, u32[]{:S(2)}, u32[]{:S(2)}) collective-permute-start(bf16[1552,128]{1,0:T(8,128)(2,1)} %get-tuple-element.12.refs_1_), channel_id=1, source_target_pairs={{1,0},{2,1},{3,2},{4,3},{5,4},{6,5},{7,6},{8,7},{9,8},{10,9},{11,1... | collective-permute-start | bytes 1191944 | tf_op jit(solution)/shard_map/ppermute | solution.py:69
  52.3 26.0 %collective-permute-start.10 = (bf16[1552,128]{1,0:T(8,128)(2,1)S(1)}, bf16[1552,128]{1,0:T(8,128)(2,1)S(1)}, u32[]{:S(2)}, u32[]{:S(2)}) collective-permute-start(bf16[1552,128]{1,0:T(8,128)(2,1)S(1)} %collective-permute-done.5.refs_3_), channel_id=1, source_target_pairs={{160,128},{161,129},{162,130},{163,131},{164,132},{165,133},{166,1... | collective-permute-start | bytes 1191944 | tf_op jit(solution)/shard_map/ppermute | solution.py:69
  53.0 25.3 %collective-permute-start.11 = (bf16[1552,128]{1,0:T(8,128)(2,1)S(1)}, bf16[1552,128]{1,0:T(8,128)(2,1)S(1)}, u32[]{:S(2)}, u32[]{:S(2)}) collective-permute-start(bf16[1552,128]{1,0:T(8,128)(2,1)S(1)} %collective-permute-done.6.refs_4_), channel_id=1, source_target_pairs={{1,0},{2,1},{3,2},{4,3},{5,4},{6,5},{7,6},{8,7},{9,8},{10,9},{11,1... | collective-permute-start | bytes 1191944 | tf_op jit(solution)/shard_map/ppermute | solution.py:69
  53.8 24.6 %collective-permute-start.9 = (bf16[1552,128]{1,0:T(8,128)(2,1)S(1)}, bf16[1552,128]{1,0:T(8,128)(2,1)S(1)}, u32[]{:S(2)}, u32[]{:S(2)}) collective-permute-start(bf16[1552,128]{1,0:T(8,128)(2,1)S(1)} %pad_maximum_fusion), channel_id=1, source_target_pairs={{32,0},{33,1},{34,2},{35,3},{36,4},{37,5},{38,6},{39,7},{40,8},{41... | collective-permute-start | bytes 1191944 | tf_op jit(solution)/shard_map/ppermute | solution.py:69
  65.1 13.2 %collective-permute-start.13 = (bf16[1552,128]{1,0:T(8,128)(2,1)S(1)}, bf16[1552,128]{1,0:T(8,128)(2,1)S(1)}, u32[]{:S(2)}, u32[]{:S(2)}) collective-permute-start(bf16[1552,128]{1,0:T(8,128)(2,1)S(1)} %collective-permute-done.8.refs_5_), channel_id=1, source_target_pairs={{14,15},{46,47},{78,79},{110,111},{142,143},{174,175},{30,31},{62,... | collective-permute-start | bytes 1191944 | tf_op jit(solution)/shard_map/ppermute | solution.py:69
  66.4 12.4 %collective-permute-start.12 = (bf16[1552,128]{1,0:T(8,128)(2,1)S(1)}, bf16[1552,128]{1,0:T(8,128)(2,1)S(1)}, u32[]{:S(2)}, u32[]{:S(2)}) collective-permute-start(bf16[1552,128]{1,0:T(8,128)(2,1)S(1)} %collective-permute-done.8.refs_5_), channel_id=1, source_target_pairs={{14,13},{15,14},{12,15},{46,45},{47,46},{44,47},{78,77},{79,78},{7... | collective-permute-start | bytes 1191944 | tf_op jit(solution)/shard_map/ppermute | solution.py:69
  73.9 1.0 %copy-start = (bf16[1552,128]{1,0:T(8,128)(2,1)S(1)}, bf16[1552,128]{1,0:T(8,128)(2,1)}, u32[]{:S(2)}) copy-start(bf16[1552,128]{1,0:T(8,128)(2,1)} %get-tuple-element.11.refs_0_) | copy-start | bytes 1191940
  74.9 1.0 %copy-start.1 = (bf16[1552,128]{1,0:T(8,128)(2,1)S(1)}, bf16[1552,128]{1,0:T(8,128)(2,1)}, u32[]{:S(2)}) copy-start(bf16[1552,128]{1,0:T(8,128)(2,1)} %get-tuple-element.12.refs_1_) | copy-start | bytes 1191940

commit v3 on v2

--- a/solution.py
+++ b/solution.py
@@ -41,6 +41,38 @@
         for z in range(Z)
         for (y, core), (to_y, to_core), dz in routes
     ]
+
+
+HOME = ((0, 0), (0, 1), (1, 0))
+VIA = (((0, 1), (7, 1), (1, 1)), ((6, 1), (5, 1), (2, 1)))
+GOAL = ((7, 0), (7, 1), (6, 0))
+
+
+def way(z):
+    return -1 if z % 2 == 1 or z == 8 else 1
+
+
+def to_planes():
+    return [
+        (device(x, *at(z, home)), device(x, *at(z + way(z), via)))
+        for x in range(X)
+        for z in range(Z)
+        for home, via in zip(HOME, VIA[z // 2 % 2], strict=True)
+    ]
+
+
+def across():
+    return [
+        (device(x, *at(z + way(z), via)), device(x, *at(z + 6, goal)))
+        for x in range(X)
+        for z in range(Z)
+        for via, goal in zip(VIA[z // 2 % 2], GOAL, strict=True)
+    ]
+
+
+def at(z, place):
+    y, core = place
+    return y, z, core
 
 
 def over(source, target):
@@ -339,8 +371,8 @@
     first_a, first_b = send(la, ring), send(lb, ring)
     over_both = send(l0, over((1, 1), (0, 5)) + over((1, 2), (0, 4)))
     second_a, second_b = send(first_a, down(5)), send(first_b, down(5))
-    moved = send(r0, per_line(((0, 1), (7, 1), 0), ((0, 0), (0, 1), 0), ((1, 0), (1, 1), 0)))
-    crossed = send(moved, per_line(((0, 1), (7, 0), 6), ((7, 1), (7, 1), 6), ((1, 1), (6, 0), 6)))
+    moved = send(r0, to_planes())
+    crossed = send(moved, across())
     n1 = send(r0, right_hop(1, 16))
     n2 = send(r0, right_hop(2, 16))
     n3 = send(n2, right_hop(1, 14))
@@ -352,17 +384,6 @@
         1: [halves(first_a, first_b)] * 6,
         2: [halves(second_a, second_b)] * 5 + [whole(over_both)],
     }
-    total = multiply(
-        None,
-        [
-            (choose(lambda z, c: whole(l0)), choose(lambda z, c: whole(r0))),
-            (
-                choose(lambda z, c: lefts[1][z] if early(c) else None),
-                choose(lambda z, c: whole(n1) if early(c) else None),
-            ),
-        ],
-        False,
-    )
     third = send(after(jnp.concatenate([second_a, second_b]), over_both), down(4))
     changed = send(over_both, over((0, 5), (0, 4)) + over((0, 4), (0, 5)))
     lefts[3] = [whole(third)] * 4 + [whole(changed)] * 2
@@ -373,16 +394,15 @@
     def right_of(step, c):
         return whole({1: (n1, g1), 2: (n2, crossed), 3: (n3, g2)}[step][c + step >= HALF_LOOP])
 
-    steps = [
-        (choose(lambda z, c: lefts[step][z]), choose(lambda z, c: right_of(step, c))) for step in (2, 3)
-    ]
-    steps.append(
-        (
-            choose(lambda z, c: None if early(c) else lefts[1][z]),
-            choose(lambda z, c: None if early(c) else right_of(1, c)),
+    def step_of(step, when=None):
+        return (
+            choose(lambda z, c: lefts[step][z] if when is None or when(c) else None),
+            choose(lambda z, c: right_of(step, c) if when is None or when(c) else None),
         )
-    )
-    return multiply(total, steps, True)
+
+    own = (choose(lambda z, c: whole(l0)), choose(lambda z, c: whole(r0)))
+    total = multiply(None, [own, step_of(2), step_of(1, early)], False)
+    return multiply(total, [step_of(3), step_of(1, lambda c: not early(c))], True)
 
 
 def solution(mesh):

time: 85.8 us -> 76 us (0.89)
  the two profiles are of different devices: /device:TPU:185 before, /device:TPU:186 now
where the time goes in v3:
time: 76 us; the launch traced here: 75.5 us
  starting transfers between devices  42.5 us (56%)
  waiting for transfers between devices  18.8 us (25%)
  Pallas kernels  12 us (16%)
  local copies, waits for them, and re-layouts  1.99 us (3%)
    ppermute x14, starting transfers between devices, send(): return lax.ppermute(block, ('row', 'col'), route)  42.5 us
    ppermute x14, waiting for transfers between devices, send(): return lax.ppermute(block, ('row', 'col'), route)  18.8 us
    pallas_call x2, Pallas kernels, multiply(): pl.pallas_call(kernel, out_shape=jax.ShapeDtypeStruct((SIDE, SIDE), jnp.b...  8.61 us
    pallas_call x1, Pallas kernels, pack(): pl.pallas_call(pack_kernel, out_shape=tuple((jax.ShapeDtypeStruct((n, TIL...  3.4 us
    unnamed x4, local copies, waits for them, and re-layouts  1.99 us
  transfers between devices with their start and end apart: 14, of which 3 were waited for; matrix products, arithmetic and copies ran while one was open for 0% of the time, Pallas kernels for 7%

profile of v3, /device:TPU:186, one launch (start us, length us, event | category | flops | bytes accessed | tf_op | source)
XLA Modules:
  0.0 75.5 jit_solution(9801704731322501199)
XLA Ops:
  0.0 3.4 %pack.1 = (bf16[768,128]{1,0:T(8,128)(2,1)}, bf16[784,128]{1,0:T(8,128)(2,1)}, bf16[1552,128]{1,0:T(8,128)(2,1)}, bf16[1552,128]{1,0:T(8,128)(2,1)}) custom-call(s32[4,8]{1,0:T(4,128)} %bitcast.1, s32[4,8]{1,0:T(4,128)} %right_mask.1, bf16[1024,512]{1,0:T(8,128)(2,1)} %left.1, bf16[512,1024]{1,0:T(8,128)(2,1)} %right.1), custom_call_target="tpu_custom_call" | custom-call | flops 1 | bytes 1 | tf_op jit(solution)/shard_map/pack/pallas_call | solution.py:161
  3.4 0.7 collective-permute-start.6
  4.1 1.9 %collective-permute-start = (bf16[768,128]{1,0:T(8,128)(2,1)}, bf16[768,128]{1,0:T(8,128)(2,1)S(1)}, u32[]{:S(2)}, u32[]{:S(2)}) collective-permute-start(bf16[768,128]{1,0:T(8,128)(2,1)} %get-tuple-element.13), channel_id=1, source_target_pairs={{32,0},{33,1},{34,2},{35,3},{36,4},{37,5},{38,6},{39,7},{40,8},{41... | collective-permute-start | bytes 589832 | tf_op jit(solution)/shard_map/ppermute | solution.py:101
  6.0 1.9 %collective-permute-start.2 = (bf16[784,128]{1,0:T(8,128)(2,1)}, bf16[784,128]{1,0:T(8,128)(2,1)S(1)}, u32[]{:S(2)}, u32[]{:S(2)}) collective-permute-start(bf16[784,128]{1,0:T(8,128)(2,1)} %get-tuple-element.14), channel_id=1, source_target_pairs={{32,0},{33,1},{34,2},{35,3},{36,4},{37,5},{38,6},{39,7},{40,8},{41... | collective-permute-start | bytes 602120 | tf_op jit(solution)/shard_map/ppermute | solution.py:101
  8.0 7.3 %collective-permute-start.4 = (bf16[1552,128]{1,0:T(8,128)(2,1)}, bf16[1552,128]{1,0:T(8,128)(2,1)S(1)}, u32[]{:S(2)}, u32[]{:S(2)}) collective-permute-start(bf16[1552,128]{1,0:T(8,128)(2,1)} %get-tuple-element.11.refs_0_), channel_id=1, source_target_pairs={{224,160},{225,161},{226,162},{227,163},{228,164},{229,165},{230,1... | collective-permute-start | bytes 1191944 | tf_op jit(solution)/shard_map/ppermute | solution.py:101
  15.3 3.3 %collective-permute-start.5 = (bf16[1552,128]{1,0:T(8,128)(2,1)}, bf16[1552,128]{1,0:T(8,128)(2,1)S(1)}, u32[]{:S(2)}, u32[]{:S(2)}) collective-permute-start(bf16[1552,128]{1,0:T(8,128)(2,1)} %get-tuple-element.12.refs_1_), channel_id=1, source_target_pairs={{2,0},{3,1},{4,2},{5,3},{6,4},{7,5},{8,6},{9,7},{10,8},{11,9},{12,... | collective-permute-start | bytes 1191944 | tf_op jit(solution)/shard_map/ppermute | solution.py:101
  18.5 0.0 collective-permute-done.refs_7_.refs_5_
  18.6 6.0 %collective-permute-start.1 = (bf16[768,128]{1,0:T(8,128)(2,1)S(1)}, bf16[768,128]{1,0:T(8,128)(2,1)S(1)}, u32[]{:S(2)}, u32[]{:S(2)}) collective-permute-start(bf16[768,128]{1,0:T(8,128)(2,1)S(1)} %collective-permute-done.refs_7_.refs_5_), channel_id=1, source_target_pairs={{32,0},{33,1},{34,2},{35,3},{36,4},{37,5},{38,6},{39,7},{40,8},{41... | collective-permute-start | bytes 589832 | tf_op jit(solution)/shard_map/ppermute | solution.py:101
  24.6 0.0 collective-permute-done.2.refs_8_.refs_6_
  24.6 1.9 %collective-permute-start.3 = (bf16[784,128]{1,0:T(8,128)(2,1)S(1)}, bf16[784,128]{1,0:T(8,128)(2,1)S(1)}, u32[]{:S(2)}, u32[]{:S(2)}) collective-permute-start(bf16[784,128]{1,0:T(8,128)(2,1)S(1)} %collective-permute-done.2.refs_8_.refs_6_), channel_id=1, source_target_pairs={{32,0},{33,1},{34,2},{35,3},{36,4},{37,5},{38,6},{39,7},{40,8},{41... | collective-permute-start | bytes 602120 | tf_op jit(solution)/shard_map/ppermute | solution.py:101
  26.5 0.0 collective-permute-done.6
  26.5 1.3 %collective-permute-start.7 = (bf16[1552,128]{1,0:T(8,128)(2,1)S(1)}, bf16[1552,128]{1,0:T(8,128)(2,1)S(1)}, u32[]{:S(2)}, u32[]{:S(2)}) collective-permute-start(bf16[1552,128]{1,0:T(8,128)(2,1)S(1)} %collective-permute-done.6), channel_id=1, source_target_pairs={{33,30},{47,31},{35,28},{1,62},{15,63},{3,60},{109,94},{107,95},{1... | collective-permute-start | bytes 1191944 | tf_op jit(solution)/shard_map/ppermute | solution.py:101
  27.8 2.1 %collective-permute-done.1.refs_2_ = bf16[768,128]{1,0:T(8,128)(2,1)S(1)} collective-permute-done((bf16[768,128]{1,0:T(8,128)(2,1)S(1)}, bf16[768,128]{1,0:T(8,128)(2,1)S(1)}, u32[]{:S(2)}, u32[]{:S(2)}) %collective-permute-start.1) | collective-permute-done | bytes 196640 | tf_op jit(solution)/shard_map/ppermute | solution.py:101
  29.9 10.6 %collective-permute-start.8 = (bf16[1552,128]{1,0:T(8,128)(2,1)}, bf16[1552,128]{1,0:T(8,128)(2,1)S(1)}, u32[]{:S(2)}, u32[]{:S(2)}) collective-permute-start(bf16[1552,128]{1,0:T(8,128)(2,1)} %get-tuple-element.12.refs_1_), channel_id=1, source_target_pairs={{1,0},{2,1},{3,2},{4,3},{5,4},{6,5},{7,6},{8,7},{9,8},{10,9},{11,1... | collective-permute-start | bytes 1191944 | tf_op jit(solution)/shard_map/ppermute | solution.py:101
  40.5 5.1 %collective-permute-done.4.refs_4_ = bf16[1552,128]{1,0:T(8,128)(2,1)S(1)} collective-permute-done((bf16[1552,128]{1,0:T(8,128)(2,1)}, bf16[1552,128]{1,0:T(8,128)(2,1)S(1)}, u32[]{:S(2)}, u32[]{:S(2)}) %collective-permute-start.4) | collective-permute-done | bytes 397344 | tf_op jit(solution)/shard_map/ppermute | solution.py:101
  45.6 0.7 collective-permute-start.10
  46.3 0.0 collective-permute-done.5.refs_5_
  46.3 0.7 collective-permute-start.11
  47.0 0.0 collective-permute-done.3.refs_3_
  47.1 1.9 %collective-permute-start.9 = (bf16[1552,128]{1,0:T(8,128)(2,1)S(1)}, bf16[1552,128]{1,0:T(8,128)(2,1)S(1)}, u32[]{:S(2)}, u32[]{:S(2)}) collective-permute-start(bf16[1552,128]{1,0:T(8,128)(2,1)S(1)} %pad_maximum_fusion), channel_id=1, source_target_pairs={{32,0},{33,1},{34,2},{35,3},{36,4},{37,5},{38,6},{39,7},{40,8},{41... | collective-permute-start | bytes 1191944 | tf_op jit(solution)/shard_map/ppermute | solution.py:101
  49.0 11.5 %collective-permute-done.7.refs_6_ = bf16[1552,128]{1,0:T(8,128)(2,1)S(1)} collective-permute-done((bf16[1552,128]{1,0:T(8,128)(2,1)S(1)}, bf16[1552,128]{1,0:T(8,128)(2,1)S(1)}, u32[]{:S(2)}, u32[]{:S(2)}) %collective-permute-start.7) | collective-permute-done | bytes 397344 | tf_op jit(solution)/shard_map/ppermute | solution.py:101
  60.5 1.9 %collective-permute-start.12 = (bf16[1552,128]{1,0:T(8,128)(2,1)S(1)}, bf16[1552,128]{1,0:T(8,128)(2,1)S(1)}, u32[]{:S(2)}, u32[]{:S(2)}) collective-permute-start(bf16[1552,128]{1,0:T(8,128)(2,1)S(1)} %collective-permute-done.7.refs_6_), channel_id=1, source_target_pairs={{14,13},{15,14},{12,15},{46,45},{47,46},{44,47},{78,77},{79,78},{7... | collective-permute-start | bytes 1191944 | tf_op jit(solution)/shard_map/ppermute | solution.py:101
  62.4 0.0 collective-permute-done.8.refs_9_
  62.4 2.4 %collective-permute-start.13 = (bf16[1552,128]{1,0:T(8,128)(2,1)S(1)}, bf16[1552,128]{1,0:T(8,128)(2,1)S(1)}, u32[]{:S(2)}, u32[]{:S(2)}) collective-permute-start(bf16[1552,128]{1,0:T(8,128)(2,1)S(1)} %collective-permute-done.7.refs_6_), channel_id=1, source_target_pairs={{14,15},{46,47},{78,79},{110,111},{142,143},{174,175},{30,31},{62,... | collective-permute-start | bytes 1191944 | tf_op jit(solution)/shard_map/ppermute | solution.py:101
  64.9 0.0 copy-start
  64.9 1.0 %copy-done = bf16[1552,128]{1,0:T(8,128)(2,1)S(1)} copy-done((bf16[1552,128]{1,0:T(8,128)(2,1)S(1)}, bf16[1552,128]{1,0:T(8,128)(2,1)}, u32[]{:S(2)}) %copy-start) | copy-done | bytes 397336
  65.9 0.0 copy-start.1
  65.9 1.0 %copy-done.1 = bf16[1552,128]{1,0:T(8,128)(2,1)S(1)} copy-done((bf16[1552,128]{1,0:T(8,128)(2,1)S(1)}, bf16[1552,128]{1,0:T(8,128)(2,1)}, u32[]{:S(2)}) %copy-start.1) | copy-done | bytes 397336
  66.9 5.3 %multiply.1.refs_0_ = f32[1024,1024]{1,0:T(8,128)S(1)} custom-call(bf16[1552,128]{1,0:T(8,128)(2,1)S(1)} %copy-done, bf16[1552,128]{1,0:T(8,128)(2,1)S(1)} %copy-done.1, bf16[768,128]{1,0:T(8,128)(2,1)S(1)} %collective-permute-done.1.refs_2_, bf16[784,128]{1,0:T(8,128)(2,1)S(1)} %collective-permute-done.3.refs_3_, ...), custom_call_target="tpu_custom_call" | custom-call | flops 1 | bytes 1 | tf_op jit(solution)/shard_map/multiply/pallas_call | solution.py:355
  72.1 0.0 collective-permute-done.10.refs_2_
  72.2 0.0 collective-permute-done.11.refs_3_
  72.2 0.0 collective-permute-done.9.refs_1_
  72.2 0.0 collective-permute-done.12.refs_4_
  72.2 0.0 collective-permute-done.13.refs_7_
  72.2 3.3 %finish.1 = bf16[1024,1024]{1,0:T(8,128)(2,1)} custom-call(f32[1024,1024]{1,0:T(8,128)S(1)} %multiply.1.refs_0_, bf16[1552,128]{1,0:T(8,128)(2,1)S(1)} %collective-permute-done.9.refs_1_, bf16[1552,128]{1,0:T(8,128)(2,1)S(1)} %collective-permute-done.10.refs_2_, bf16[1552,128]{1,0:T(8,128)(2,1)S(1)} %collective-permute-done.11.refs_3_, ...), custom_call_target="tpu_custom_call" | custom-call | flops 1 | bytes 1 | tf_op jit(solution)/shard_map/finish/pallas_call | solution.py:355
  (1 shorter events, 0.0 us)
Async XLA Ops:
  3.4 23.1 %collective-permute-start.6 = (bf16[1552,128]{1,0:T(8,128)(2,1)}, bf16[1552,128]{1,0:T(8,128)(2,1)S(1)}, u32[]{:S(2)}, u32[]{:S(2)}) collective-permute-start(bf16[1552,128]{1,0:T(8,128)(2,1)} %get-tuple-element.12.refs_1_), channel_id=1, source_target_pairs={{0,33},{1,47},{2,35},{32,1},{33,15},{34,3},{64,109},{65,107},{66,1... | collective-permute-start | bytes 1191944 | tf_op jit(solution)/shard_map/ppermute | solution.py:101
  4.1 14.4 %collective-permute-start = (bf16[768,128]{1,0:T(8,128)(2,1)}, bf16[768,128]{1,0:T(8,128)(2,1)S(1)}, u32[]{:S(2)}, u32[]{:S(2)}) collective-permute-start(bf16[768,128]{1,0:T(8,128)(2,1)} %get-tuple-element.13), channel_id=1, source_target_pairs={{32,0},{33,1},{34,2},{35,3},{36,4},{37,5},{38,6},{39,7},{40,8},{41... | collective-permute-start | bytes 589832 | tf_op jit(solution)/shard_map/ppermute | solution.py:101
  6.0 18.5 %collective-permute-start.2 = (bf16[784,128]{1,0:T(8,128)(2,1)}, bf16[784,128]{1,0:T(8,128)(2,1)S(1)}, u32[]{:S(2)}, u32[]{:S(2)}) collective-permute-start(bf16[784,128]{1,0:T(8,128)(2,1)} %get-tuple-element.14), channel_id=1, source_target_pairs={{32,0},{33,1},{34,2},{35,3},{36,4},{37,5},{38,6},{39,7},{40,8},{41... | collective-permute-start | bytes 602120 | tf_op jit(solution)/shard_map/ppermute | solution.py:101
  8.0 37.7 %collective-permute-start.4 = (bf16[1552,128]{1,0:T(8,128)(2,1)}, bf16[1552,128]{1,0:T(8,128)(2,1)S(1)}, u32[]{:S(2)}, u32[]{:S(2)}) collective-permute-start(bf16[1552,128]{1,0:T(8,128)(2,1)} %get-tuple-element.11.refs_0_), channel_id=1, source_target_pairs={{224,160},{225,161},{226,162},{227,163},{228,164},{229,165},{230,1... | collective-permute-start | bytes 1191944 | tf_op jit(solution)/shard_map/ppermute | solution.py:101
  15.3 31.1 %collective-permute-start.5 = (bf16[1552,128]{1,0:T(8,128)(2,1)}, bf16[1552,128]{1,0:T(8,128)(2,1)S(1)}, u32[]{:S(2)}, u32[]{:S(2)}) collective-permute-start(bf16[1552,128]{1,0:T(8,128)(2,1)} %get-tuple-element.12.refs_1_), channel_id=1, source_target_pairs={{2,0},{3,1},{4,2},{5,3},{6,4},{7,5},{8,6},{9,7},{10,8},{11,9},{12,... | collective-permute-start | bytes 1191944 | tf_op jit(solution)/shard_map/ppermute | solution.py:101
  18.6 11.3 %collective-permute-start.1 = (bf16[768,128]{1,0:T(8,128)(2,1)S(1)}, bf16[768,128]{1,0:T(8,128)(2,1)S(1)}, u32[]{:S(2)}, u32[]{:S(2)}) collective-permute-start(bf16[768,128]{1,0:T(8,128)(2,1)S(1)} %collective-permute-done.refs_7_.refs_5_), channel_id=1, source_target_pairs={{32,0},{33,1},{34,2},{35,3},{36,4},{37,5},{38,6},{39,7},{40,8},{41... | collective-permute-start | bytes 589832 | tf_op jit(solution)/shard_map/ppermute | solution.py:101
  24.6 22.4 %collective-permute-start.3 = (bf16[784,128]{1,0:T(8,128)(2,1)S(1)}, bf16[784,128]{1,0:T(8,128)(2,1)S(1)}, u32[]{:S(2)}, u32[]{:S(2)}) collective-permute-start(bf16[784,128]{1,0:T(8,128)(2,1)S(1)} %collective-permute-done.2.refs_8_.refs_6_), channel_id=1, source_target_pairs={{32,0},{33,1},{34,2},{35,3},{36,4},{37,5},{38,6},{39,7},{40,8},{41... | collective-permute-start | bytes 602120 | tf_op jit(solution)/shard_map/ppermute | solution.py:101
  26.5 34.0 %collective-permute-start.7 = (bf16[1552,128]{1,0:T(8,128)(2,1)S(1)}, bf16[1552,128]{1,0:T(8,128)(2,1)S(1)}, u32[]{:S(2)}, u32[]{:S(2)}) collective-permute-start(bf16[1552,128]{1,0:T(8,128)(2,1)S(1)} %collective-permute-done.6), channel_id=1, source_target_pairs={{33,30},{47,31},{35,28},{1,62},{15,63},{3,60},{109,94},{107,95},{1... | collective-permute-start | bytes 1191944 | tf_op jit(solution)/shard_map/ppermute | solution.py:101
  29.9 32.5 %collective-permute-start.8 = (bf16[1552,128]{1,0:T(8,128)(2,1)}, bf16[1552,128]{1,0:T(8,128)(2,1)S(1)}, u32[]{:S(2)}, u32[]{:S(2)}) collective-permute-start(bf16[1552,128]{1,0:T(8,128)(2,1)} %get-tuple-element.12.refs_1_), channel_id=1, source_target_pairs={{1,0},{2,1},{3,2},{4,3},{5,4},{6,5},{7,6},{8,7},{9,8},{10,9},{11,1... | collective-permute-start | bytes 1191944 | tf_op jit(solution)/shard_map/ppermute | solution.py:101
  45.6 26.5 %collective-permute-start.10 = (bf16[1552,128]{1,0:T(8,128)(2,1)S(1)}, bf16[1552,128]{1,0:T(8,128)(2,1)S(1)}, u32[]{:S(2)}, u32[]{:S(2)}) collective-permute-start(bf16[1552,128]{1,0:T(8,128)(2,1)S(1)} %collective-permute-done.4.refs_4_), channel_id=1, source_target_pairs={{160,128},{161,129},{162,130},{163,131},{164,132},{165,133},{166,1... | collective-permute-start | bytes 1191944 | tf_op jit(solution)/shard_map/ppermute | solution.py:101
  46.3 25.8 %collective-permute-start.11 = (bf16[1552,128]{1,0:T(8,128)(2,1)S(1)}, bf16[1552,128]{1,0:T(8,128)(2,1)S(1)}, u32[]{:S(2)}, u32[]{:S(2)}) collective-permute-start(bf16[1552,128]{1,0:T(8,128)(2,1)S(1)} %collective-permute-done.5.refs_5_), channel_id=1, source_target_pairs={{1,0},{2,1},{3,2},{4,3},{5,4},{6,5},{7,6},{8,7},{9,8},{10,9},{11,1... | collective-permute-start | bytes 1191944 | tf_op jit(solution)/shard_map/ppermute | solution.py:101
  47.1 25.1 %collective-permute-start.9 = (bf16[1552,128]{1,0:T(8,128)(2,1)S(1)}, bf16[1552,128]{1,0:T(8,128)(2,1)S(1)}, u32[]{:S(2)}, u32[]{:S(2)}) collective-permute-start(bf16[1552,128]{1,0:T(8,128)(2,1)S(1)} %pad_maximum_fusion), channel_id=1, source_target_pairs={{32,0},{33,1},{34,2},{35,3},{36,4},{37,5},{38,6},{39,7},{40,8},{41... | collective-permute-start | bytes 1191944 | tf_op jit(solution)/shard_map/ppermute | solution.py:101
  60.5 11.7 %collective-permute-start.12 = (bf16[1552,128]{1,0:T(8,128)(2,1)S(1)}, bf16[1552,128]{1,0:T(8,128)(2,1)S(1)}, u32[]{:S(2)}, u32[]{:S(2)}) collective-permute-start(bf16[1552,128]{1,0:T(8,128)(2,1)S(1)} %collective-permute-done.7.refs_6_), channel_id=1, source_target_pairs={{14,13},{15,14},{12,15},{46,45},{47,46},{44,47},{78,77},{79,78},{7... | collective-permute-start | bytes 1191944 | tf_op jit(solution)/shard_map/ppermute | solution.py:101
  62.4 9.8 %collective-permute-start.13 = (bf16[1552,128]{1,0:T(8,128)(2,1)S(1)}, bf16[1552,128]{1,0:T(8,128)(2,1)S(1)}, u32[]{:S(2)}, u32[]{:S(2)}) collective-permute-start(bf16[1552,128]{1,0:T(8,128)(2,1)S(1)} %collective-permute-done.7.refs_6_), channel_id=1, source_target_pairs={{14,15},{46,47},{78,79},{110,111},{142,143},{174,175},{30,31},{62,... | collective-permute-start | bytes 1191944 | tf_op jit(solution)/shard_map/ppermute | solution.py:101
  64.9 1.0 %copy-start = (bf16[1552,128]{1,0:T(8,128)(2,1)S(1)}, bf16[1552,128]{1,0:T(8,128)(2,1)}, u32[]{:S(2)}) copy-start(bf16[1552,128]{1,0:T(8,128)(2,1)} %get-tuple-element.11.refs_0_) | copy-start | bytes 1191940
  65.9 1.0 %copy-start.1 = (bf16[1552,128]{1,0:T(8,128)(2,1)S(1)}, bf16[1552,128]{1,0:T(8,128)(2,1)}, u32[]{:S(2)}) copy-start(bf16[1552,128]{1,0:T(8,128)(2,1)} %get-tuple-element.12.refs_1_) | copy-start | bytes 1191940

commit v4 on v3

--- a/solution.py
+++ b/solution.py
@@ -44,12 +44,16 @@
 
 
 HOME = ((0, 0), (0, 1), (1, 0))
-VIA = (((0, 1), (7, 1), (1, 1)), ((6, 1), (5, 1), (2, 1)))
+VIA = (((0, 1), (7, 1), (1, 1)), ((6, 1), (5, 1), (2, 1)), ((3, 1), (4, 1), (3, 0)))
 GOAL = ((7, 0), (7, 1), (6, 0))
 
 
 def way(z):
     return -1 if z % 2 == 1 or z == 8 else 1
+
+
+def planes(z):
+    return 2 if z in (8, 9) else z // 2 % 2
 
 
 def to_planes():
@@ -57,7 +61,7 @@
         (device(x, *at(z, home)), device(x, *at(z + way(z), via)))
         for x in range(X)
         for z in range(Z)
-        for home, via in zip(HOME, VIA[z // 2 % 2], strict=True)
+        for home, via in zip(HOME, VIA[planes(z)], strict=True)
     ]
 
 
@@ -66,7 +70,7 @@
         (device(x, *at(z + way(z), via)), device(x, *at(z + 6, goal)))
         for x in range(X)
         for z in range(Z)
-        for via, goal in zip(VIA[z // 2 % 2], GOAL, strict=True)
+        for via, goal in zip(VIA[planes(z)], GOAL, strict=True)
     ]
 
 

time: 76 us -> 75.7 us (level)
  the two profiles are of different devices: /device:TPU:186 before, /device:TPU:185 now
where the time goes in v4:
time: 75.7 us; the launch traced here: 74.8 us
  starting transfers between devices  47 us (62%)
  waiting for transfers between devices  13.4 us (18%)
  Pallas kernels  12.1 us (16%)
  local copies, waits for them, and re-layouts  1.99 us (3%)
    ppermute x14, starting transfers between devices, send(): return lax.ppermute(block, ('row', 'col'), route)  47 us
    ppermute x14, waiting for transfers between devices, send(): return lax.ppermute(block, ('row', 'col'), route)  13.4 us
    pallas_call x2, Pallas kernels, multiply(): pl.pallas_call(kernel, out_shape=jax.ShapeDtypeStruct((SIDE, SIDE), jnp.b...  8.68 us
    pallas_call x1, Pallas kernels, pack(): pl.pallas_call(pack_kernel, out_shape=tuple((jax.ShapeDtypeStruct((n, TIL...  3.4 us
    unnamed x4, local copies, waits for them, and re-layouts  1.99 us
  transfers between devices with their start and end apart: 14, of which 1 were waited for; matrix products, arithmetic and copies ran while one was open for 0% of the time, Pallas kernels for 5%

profile of v4, /device:TPU:185, one launch (start us, length us, event | category | flops | bytes accessed | tf_op | source)
XLA Modules:
  0.0 74.8 jit_solution(5633524383740162842)
XLA Ops:
  0.0 3.4 %pack.1 = (bf16[768,128]{1,0:T(8,128)(2,1)}, bf16[784,128]{1,0:T(8,128)(2,1)}, bf16[1552,128]{1,0:T(8,128)(2,1)}, bf16[1552,128]{1,0:T(8,128)(2,1)}) custom-call(s32[4,8]{1,0:T(4,128)} %bitcast.1, s32[4,8]{1,0:T(4,128)} %right_mask.1, bf16[1024,512]{1,0:T(8,128)(2,1)} %left.1, bf16[512,1024]{1,0:T(8,128)(2,1)} %right.1), custom_call_target="tpu_custom_call" | custom-call | flops 1 | bytes 1 | tf_op jit(solution)/shard_map/pack/pallas_call | solution.py:165
  3.4 0.7 collective-permute-start.6
  4.1 1.9 %collective-permute-start = (bf16[768,128]{1,0:T(8,128)(2,1)}, bf16[768,128]{1,0:T(8,128)(2,1)S(1)}, u32[]{:S(2)}, u32[]{:S(2)}) collective-permute-start(bf16[768,128]{1,0:T(8,128)(2,1)} %get-tuple-element.13), channel_id=1, source_target_pairs={{32,0},{33,1},{34,2},{35,3},{36,4},{37,5},{38,6},{39,7},{40,8},{41... | collective-permute-start | bytes 589832 | tf_op jit(solution)/shard_map/ppermute | solution.py:105
  6.0 1.9 %collective-permute-start.2 = (bf16[784,128]{1,0:T(8,128)(2,1)}, bf16[784,128]{1,0:T(8,128)(2,1)S(1)}, u32[]{:S(2)}, u32[]{:S(2)}) collective-permute-start(bf16[784,128]{1,0:T(8,128)(2,1)} %get-tuple-element.14), channel_id=1, source_target_pairs={{32,0},{33,1},{34,2},{35,3},{36,4},{37,5},{38,6},{39,7},{40,8},{41... | collective-permute-start | bytes 602120 | tf_op jit(solution)/shard_map/ppermute | solution.py:105
  8.0 9.8 %collective-permute-start.4 = (bf16[1552,128]{1,0:T(8,128)(2,1)}, bf16[1552,128]{1,0:T(8,128)(2,1)S(1)}, u32[]{:S(2)}, u32[]{:S(2)}) collective-permute-start(bf16[1552,128]{1,0:T(8,128)(2,1)} %get-tuple-element.11.refs_0_), channel_id=1, source_target_pairs={{224,160},{225,161},{226,162},{227,163},{228,164},{229,165},{230,1... | collective-permute-start | bytes 1191944 | tf_op jit(solution)/shard_map/ppermute | solution.py:105
  17.8 2.4 %collective-permute-start.5 = (bf16[1552,128]{1,0:T(8,128)(2,1)}, bf16[1552,128]{1,0:T(8,128)(2,1)S(1)}, u32[]{:S(2)}, u32[]{:S(2)}) collective-permute-start(bf16[1552,128]{1,0:T(8,128)(2,1)} %get-tuple-element.12.refs_1_), channel_id=1, source_target_pairs={{2,0},{3,1},{4,2},{5,3},{6,4},{7,5},{8,6},{9,7},{10,8},{11,9},{12,... | collective-permute-start | bytes 1191944 | tf_op jit(solution)/shard_map/ppermute | solution.py:105
  20.2 0.0 collective-permute-done.refs_7_.refs_5_
  20.2 5.4 %collective-permute-start.1 = (bf16[768,128]{1,0:T(8,128)(2,1)S(1)}, bf16[768,128]{1,0:T(8,128)(2,1)S(1)}, u32[]{:S(2)}, u32[]{:S(2)}) collective-permute-start(bf16[768,128]{1,0:T(8,128)(2,1)S(1)} %collective-permute-done.refs_7_.refs_5_), channel_id=1, source_target_pairs={{32,0},{33,1},{34,2},{35,3},{36,4},{37,5},{38,6},{39,7},{40,8},{41... | collective-permute-start | bytes 589832 | tf_op jit(solution)/shard_map/ppermute | solution.py:105
  25.7 0.0 collective-permute-done.2.refs_8_.refs_6_
  25.7 1.9 %collective-permute-start.3 = (bf16[784,128]{1,0:T(8,128)(2,1)S(1)}, bf16[784,128]{1,0:T(8,128)(2,1)S(1)}, u32[]{:S(2)}, u32[]{:S(2)}) collective-permute-start(bf16[784,128]{1,0:T(8,128)(2,1)S(1)} %collective-permute-done.2.refs_8_.refs_6_), channel_id=1, source_target_pairs={{32,0},{33,1},{34,2},{35,3},{36,4},{37,5},{38,6},{39,7},{40,8},{41... | collective-permute-start | bytes 602120 | tf_op jit(solution)/shard_map/ppermute | solution.py:105
  27.6 0.0 collective-permute-done.6
  27.6 1.3 %collective-permute-start.7 = (bf16[1552,128]{1,0:T(8,128)(2,1)S(1)}, bf16[1552,128]{1,0:T(8,128)(2,1)S(1)}, u32[]{:S(2)}, u32[]{:S(2)}) collective-permute-start(bf16[1552,128]{1,0:T(8,128)(2,1)S(1)} %collective-permute-done.6), channel_id=1, source_target_pairs={{33,30},{47,31},{35,28},{1,62},{15,63},{3,60},{109,94},{107,95},{1... | collective-permute-start | bytes 1191944 | tf_op jit(solution)/shard_map/ppermute | solution.py:105
  28.9 0.0 collective-permute-done.1.refs_2_
  28.9 5.8 %collective-permute-start.8 = (bf16[1552,128]{1,0:T(8,128)(2,1)}, bf16[1552,128]{1,0:T(8,128)(2,1)S(1)}, u32[]{:S(2)}, u32[]{:S(2)}) collective-permute-start(bf16[1552,128]{1,0:T(8,128)(2,1)} %get-tuple-element.12.refs_1_), channel_id=1, source_target_pairs={{1,0},{2,1},{3,2},{4,3},{5,4},{6,5},{7,6},{8,7},{9,8},{10,9},{11,1... | collective-permute-start | bytes 1191944 | tf_op jit(solution)/shard_map/ppermute | solution.py:105
  34.7 13.4 %collective-permute-done.4.refs_4_ = bf16[1552,128]{1,0:T(8,128)(2,1)S(1)} collective-permute-done((bf16[1552,128]{1,0:T(8,128)(2,1)}, bf16[1552,128]{1,0:T(8,128)(2,1)S(1)}, u32[]{:S(2)}, u32[]{:S(2)}) %collective-permute-start.4) | collective-permute-done | bytes 397344 | tf_op jit(solution)/shard_map/ppermute | solution.py:105
  48.1 0.7 collective-permute-start.10
  48.8 0.0 collective-permute-done.5.refs_5_
  48.8 0.7 collective-permute-start.11
  49.5 0.0 collective-permute-done.3.refs_3_
  49.5 1.9 %collective-permute-start.9 = (bf16[1552,128]{1,0:T(8,128)(2,1)S(1)}, bf16[1552,128]{1,0:T(8,128)(2,1)S(1)}, u32[]{:S(2)}, u32[]{:S(2)}) collective-permute-start(bf16[1552,128]{1,0:T(8,128)(2,1)S(1)} %pad_maximum_fusion), channel_id=1, source_target_pairs={{32,0},{33,1},{34,2},{35,3},{36,4},{37,5},{38,6},{39,7},{40,8},{41... | collective-permute-start | bytes 1191944 | tf_op jit(solution)/shard_map/ppermute | solution.py:105
  51.5 0.0 collective-permute-done.7.refs_6_
  51.5 11.3 %collective-permute-start.12 = (bf16[1552,128]{1,0:T(8,128)(2,1)S(1)}, bf16[1552,128]{1,0:T(8,128)(2,1)S(1)}, u32[]{:S(2)}, u32[]{:S(2)}) collective-permute-start(bf16[1552,128]{1,0:T(8,128)(2,1)S(1)} %collective-permute-done.7.refs_6_), channel_id=1, source_target_pairs={{14,13},{15,14},{12,15},{46,45},{47,46},{44,47},{78,77},{79,78},{7... | collective-permute-start | bytes 1191944 | tf_op jit(solution)/shard_map/ppermute | solution.py:105
  62.7 0.0 collective-permute-done.8.refs_9_
  62.7 1.3 %collective-permute-start.13 = (bf16[1552,128]{1,0:T(8,128)(2,1)S(1)}, bf16[1552,128]{1,0:T(8,128)(2,1)S(1)}, u32[]{:S(2)}, u32[]{:S(2)}) collective-permute-start(bf16[1552,128]{1,0:T(8,128)(2,1)S(1)} %collective-permute-done.7.refs_6_), channel_id=1, source_target_pairs={{14,15},{46,47},{78,79},{110,111},{142,143},{174,175},{30,31},{62,... | collective-permute-start | bytes 1191944 | tf_op jit(solution)/shard_map/ppermute | solution.py:105
  64.0 0.0 copy-start
  64.1 1.0 %copy-done = bf16[1552,128]{1,0:T(8,128)(2,1)S(1)} copy-done((bf16[1552,128]{1,0:T(8,128)(2,1)S(1)}, bf16[1552,128]{1,0:T(8,128)(2,1)}, u32[]{:S(2)}) %copy-start) | copy-done | bytes 397336
  65.0 0.0 copy-start.1
  65.1 1.0 %copy-done.1 = bf16[1552,128]{1,0:T(8,128)(2,1)S(1)} copy-done((bf16[1552,128]{1,0:T(8,128)(2,1)S(1)}, bf16[1552,128]{1,0:T(8,128)(2,1)}, u32[]{:S(2)}) %copy-start.1) | copy-done | bytes 397336
  66.0 3.9 %multiply.1.refs_0_ = f32[1024,1024]{1,0:T(8,128)S(1)} custom-call(bf16[1552,128]{1,0:T(8,128)(2,1)S(1)} %copy-done, bf16[1552,128]{1,0:T(8,128)(2,1)S(1)} %copy-done.1, bf16[768,128]{1,0:T(8,128)(2,1)S(1)} %collective-permute-done.1.refs_2_, bf16[784,128]{1,0:T(8,128)(2,1)S(1)} %collective-permute-done.3.refs_3_, ...), custom_call_target="tpu_custom_call" | custom-call | flops 1 | bytes 1 | tf_op jit(solution)/shard_map/multiply/pallas_call | solution.py:359
  70.0 0.0 collective-permute-done.10.refs_2_
  70.0 0.0 collective-permute-done.11.refs_3_
  70.0 0.0 collective-permute-done.9.refs_1_
  70.0 0.0 collective-permute-done.12.refs_4_
  70.0 0.0 collective-permute-done.13.refs_7_
  70.0 4.8 %finish.1 = bf16[1024,1024]{1,0:T(8,128)(2,1)} custom-call(f32[1024,1024]{1,0:T(8,128)S(1)} %multiply.1.refs_0_, bf16[1552,128]{1,0:T(8,128)(2,1)S(1)} %collective-permute-done.9.refs_1_, bf16[1552,128]{1,0:T(8,128)(2,1)S(1)} %collective-permute-done.10.refs_2_, bf16[1552,128]{1,0:T(8,128)(2,1)S(1)} %collective-permute-done.11.refs_3_, ...), custom_call_target="tpu_custom_call" | custom-call | flops 1 | bytes 1 | tf_op jit(solution)/shard_map/finish/pallas_call | solution.py:359
  (1 shorter events, 0.0 us)
Async XLA Ops:
  3.4 24.2 %collective-permute-start.6 = (bf16[1552,128]{1,0:T(8,128)(2,1)}, bf16[1552,128]{1,0:T(8,128)(2,1)S(1)}, u32[]{:S(2)}, u32[]{:S(2)}) collective-permute-start(bf16[1552,128]{1,0:T(8,128)(2,1)} %get-tuple-element.12.refs_1_), channel_id=1, source_target_pairs={{0,33},{1,47},{2,35},{32,1},{33,15},{34,3},{64,109},{65,107},{66,1... | collective-permute-start | bytes 1191944 | tf_op jit(solution)/shard_map/ppermute | solution.py:105
  4.1 16.1 %collective-permute-start = (bf16[768,128]{1,0:T(8,128)(2,1)}, bf16[768,128]{1,0:T(8,128)(2,1)S(1)}, u32[]{:S(2)}, u32[]{:S(2)}) collective-permute-start(bf16[768,128]{1,0:T(8,128)(2,1)} %get-tuple-element.13), channel_id=1, source_target_pairs={{32,0},{33,1},{34,2},{35,3},{36,4},{37,5},{38,6},{39,7},{40,8},{41... | collective-permute-start | bytes 589832 | tf_op jit(solution)/shard_map/ppermute | solution.py:105
  6.0 19.6 %collective-permute-start.2 = (bf16[784,128]{1,0:T(8,128)(2,1)}, bf16[784,128]{1,0:T(8,128)(2,1)S(1)}, u32[]{:S(2)}, u32[]{:S(2)}) collective-permute-start(bf16[784,128]{1,0:T(8,128)(2,1)} %get-tuple-element.14), channel_id=1, source_target_pairs={{32,0},{33,1},{34,2},{35,3},{36,4},{37,5},{38,6},{39,7},{40,8},{41... | collective-permute-start | bytes 602120 | tf_op jit(solution)/shard_map/ppermute | solution.py:105
  8.0 40.1 %collective-permute-start.4 = (bf16[1552,128]{1,0:T(8,128)(2,1)}, bf16[1552,128]{1,0:T(8,128)(2,1)S(1)}, u32[]{:S(2)}, u32[]{:S(2)}) collective-permute-start(bf16[1552,128]{1,0:T(8,128)(2,1)} %get-tuple-element.11.refs_0_), channel_id=1, source_target_pairs={{224,160},{225,161},{226,162},{227,163},{228,164},{229,165},{230,1... | collective-permute-start | bytes 1191944 | tf_op jit(solution)/shard_map/ppermute | solution.py:105
  17.8 31.0 %collective-permute-start.5 = (bf16[1552,128]{1,0:T(8,128)(2,1)}, bf16[1552,128]{1,0:T(8,128)(2,1)S(1)}, u32[]{:S(2)}, u32[]{:S(2)}) collective-permute-start(bf16[1552,128]{1,0:T(8,128)(2,1)} %get-tuple-element.12.refs_1_), channel_id=1, source_target_pairs={{2,0},{3,1},{4,2},{5,3},{6,4},{7,5},{8,6},{9,7},{10,8},{11,9},{12,... | collective-permute-start | bytes 1191944 | tf_op jit(solution)/shard_map/ppermute | solution.py:105
  20.2 8.7 %collective-permute-start.1 = (bf16[768,128]{1,0:T(8,128)(2,1)S(1)}, bf16[768,128]{1,0:T(8,128)(2,1)S(1)}, u32[]{:S(2)}, u32[]{:S(2)}) collective-permute-start(bf16[768,128]{1,0:T(8,128)(2,1)S(1)} %collective-permute-done.refs_7_.refs_5_), channel_id=1, source_target_pairs={{32,0},{33,1},{34,2},{35,3},{36,4},{37,5},{38,6},{39,7},{40,8},{41... | collective-permute-start | bytes 589832 | tf_op jit(solution)/shard_map/ppermute | solution.py:105
  25.7 23.8 %collective-permute-start.3 = (bf16[784,128]{1,0:T(8,128)(2,1)S(1)}, bf16[784,128]{1,0:T(8,128)(2,1)S(1)}, u32[]{:S(2)}, u32[]{:S(2)}) collective-permute-start(bf16[784,128]{1,0:T(8,128)(2,1)S(1)} %collective-permute-done.2.refs_8_.refs_6_), channel_id=1, source_target_pairs={{32,0},{33,1},{34,2},{35,3},{36,4},{37,5},{38,6},{39,7},{40,8},{41... | collective-permute-start | bytes 602120 | tf_op jit(solution)/shard_map/ppermute | solution.py:105
  27.6 23.8 %collective-permute-start.7 = (bf16[1552,128]{1,0:T(8,128)(2,1)S(1)}, bf16[1552,128]{1,0:T(8,128)(2,1)S(1)}, u32[]{:S(2)}, u32[]{:S(2)}) collective-permute-start(bf16[1552,128]{1,0:T(8,128)(2,1)S(1)} %collective-permute-done.6), channel_id=1, source_target_pairs={{33,30},{47,31},{35,28},{1,62},{15,63},{3,60},{109,94},{107,95},{1... | collective-permute-start | bytes 1191944 | tf_op jit(solution)/shard_map/ppermute | solution.py:105
  28.9 33.8 %collective-permute-start.8 = (bf16[1552,128]{1,0:T(8,128)(2,1)}, bf16[1552,128]{1,0:T(8,128)(2,1)S(1)}, u32[]{:S(2)}, u32[]{:S(2)}) collective-permute-start(bf16[1552,128]{1,0:T(8,128)(2,1)} %get-tuple-element.12.refs_1_), channel_id=1, source_target_pairs={{1,0},{2,1},{3,2},{4,3},{5,4},{6,5},{7,6},{8,7},{9,8},{10,9},{11,1... | collective-permute-start | bytes 1191944 | tf_op jit(solution)/shard_map/ppermute | solution.py:105
  48.1 21.9 %collective-permute-start.10 = (bf16[1552,128]{1,0:T(8,128)(2,1)S(1)}, bf16[1552,128]{1,0:T(8,128)(2,1)S(1)}, u32[]{:S(2)}, u32[]{:S(2)}) collective-permute-start(bf16[1552,128]{1,0:T(8,128)(2,1)S(1)} %collective-permute-done.4.refs_4_), channel_id=1, source_target_pairs={{160,128},{161,129},{162,130},{163,131},{164,132},{165,133},{166,1... | collective-permute-start | bytes 1191944 | tf_op jit(solution)/shard_map/ppermute | solution.py:105
  48.8 21.2 %collective-permute-start.11 = (bf16[1552,128]{1,0:T(8,128)(2,1)S(1)}, bf16[1552,128]{1,0:T(8,128)(2,1)S(1)}, u32[]{:S(2)}, u32[]{:S(2)}) collective-permute-start(bf16[1552,128]{1,0:T(8,128)(2,1)S(1)} %collective-permute-done.5.refs_5_), channel_id=1, source_target_pairs={{1,0},{2,1},{3,2},{4,3},{5,4},{6,5},{7,6},{8,7},{9,8},{10,9},{11,1... | collective-permute-start | bytes 1191944 | tf_op jit(solution)/shard_map/ppermute | solution.py:105
  49.5 20.5 %collective-permute-start.9 = (bf16[1552,128]{1,0:T(8,128)(2,1)S(1)}, bf16[1552,128]{1,0:T(8,128)(2,1)S(1)}, u32[]{:S(2)}, u32[]{:S(2)}) collective-permute-start(bf16[1552,128]{1,0:T(8,128)(2,1)S(1)} %pad_maximum_fusion), channel_id=1, source_target_pairs={{32,0},{33,1},{34,2},{35,3},{36,4},{37,5},{38,6},{39,7},{40,8},{41... | collective-permute-start | bytes 1191944 | tf_op jit(solution)/shard_map/ppermute | solution.py:105
  51.5 18.6 %collective-permute-start.12 = (bf16[1552,128]{1,0:T(8,128)(2,1)S(1)}, bf16[1552,128]{1,0:T(8,128)(2,1)S(1)}, u32[]{:S(2)}, u32[]{:S(2)}) collective-permute-start(bf16[1552,128]{1,0:T(8,128)(2,1)S(1)} %collective-permute-done.7.refs_6_), channel_id=1, source_target_pairs={{14,13},{15,14},{12,15},{46,45},{47,46},{44,47},{78,77},{79,78},{7... | collective-permute-start | bytes 1191944 | tf_op jit(solution)/shard_map/ppermute | solution.py:105
  62.7 7.3 %collective-permute-start.13 = (bf16[1552,128]{1,0:T(8,128)(2,1)S(1)}, bf16[1552,128]{1,0:T(8,128)(2,1)S(1)}, u32[]{:S(2)}, u32[]{:S(2)}) collective-permute-start(bf16[1552,128]{1,0:T(8,128)(2,1)S(1)} %collective-permute-done.7.refs_6_), channel_id=1, source_target_pairs={{14,15},{46,47},{78,79},{110,111},{142,143},{174,175},{30,31},{62,... | collective-permute-start | bytes 1191944 | tf_op jit(solution)/shard_map/ppermute | solution.py:105
  64.0 1.0 %copy-start = (bf16[1552,128]{1,0:T(8,128)(2,1)S(1)}, bf16[1552,128]{1,0:T(8,128)(2,1)}, u32[]{:S(2)}) copy-start(bf16[1552,128]{1,0:T(8,128)(2,1)} %get-tuple-element.11.refs_0_) | copy-start | bytes 1191940
  65.0 1.0 %copy-start.1 = (bf16[1552,128]{1,0:T(8,128)(2,1)S(1)}, bf16[1552,128]{1,0:T(8,128)(2,1)}, u32[]{:S(2)}) copy-start(bf16[1552,128]{1,0:T(8,128)(2,1)} %get-tuple-element.12.refs_1_) | copy-start | bytes 1191940
